TPU v7x, 128 devices: a whole 4x4x4 slice. The times are simulated.
128 devices in a mesh: slab: 2 (over z_hi), row: 4 (over z_lo, core), col: 16 (over x, y).
Axes of the slice: x: 4, y: 4, z: 4 (z_hi: 2, z_lo: 2; z = z_hi * 2 + z_lo), core: 2. Of those that a mesh axis runs over, the one named last changes fastest.
Arguments:
- distances: bfloat16 [1024, 4096], P(('slab', 'row', 'col')), may hold values from 0.19921875 to 2
- projection: bfloat16 [4096, 4, 2, 2048], P(None, None, None, 'col'), may hold values from -0.25 to 0.25
- phases: float32 [4, 2, 2048], P(None, None, 'col'), may hold values from -3.140625 to 3.140625
- segment_ids: int32 [1024], replicated, may hold values from 0 to 7, never falling along the last dimension, each value on 1 to 192 neighbouring positions
Outputs:
- instant_cov: float32 [16384, 4, 2, 2048], P('row', None, 'slab', 'col')
- lagged_cov: float32 [16384, 4, 2, 2048], P('row', None, 'slab', 'col')
Inputs may be any that keep to these rules, and one draw needn't show every extreme that they name: `segment_ids`: segment ids never fall along the frames; each segment holds 1 to 192 frames and one holds exactly 192.
All inputs are finite; a program needn't handle non-finite values.
Results may differ from a plain program's by a relative error of at most 0.0011.
Values may be sent and summed in bfloat16 or wider, within the bound.
A program may use at most 192 MiB of HBM per device.

v0:
```python
import jax
import jax.numpy as jnp
from jax import lax
from jax.sharding import PartitionSpec as P

LAG = 50


def per_device(distances, projection, phases, segment_ids):
    n_slab = lax.axis_size("slab")
    row_index = lax.axis_index("row")
    input_width = projection.shape[0]
    n_row = projection.shape[1]
    n_part = projection.shape[2]
    part_width = projection.shape[3]
    local_width = n_row * n_part * part_width
    frame_rows = lax.all_gather(distances, "col", axis=0, tiled=True)
    flat_projection = projection.reshape(input_width, local_width)
    angles = jnp.dot(
        frame_rows, flat_projection, preferred_element_type=jnp.float32
    ) + phases.reshape(1, local_width)
    own_features = jnp.cos(angles).astype(jnp.bfloat16)
    right_block = lax.all_gather(own_features, "row", axis=0, tiled=True)
    frame_count = right_block.shape[0]
    row_parts = right_block.reshape(frame_count, n_row, n_part * part_width)
    own_rows = lax.dynamic_index_in_dim(row_parts, row_index, 1, keepdims=False)
    own_rows = own_rows.reshape(frame_count, n_part, part_width)
    left_block = lax.all_gather(own_rows, "col", axis=2, tiled=True)
    left_block = left_block.reshape(frame_count, -1)
    tile_height = left_block.shape[1]
    segment_next = jnp.concatenate([segment_ids[LAG:], jnp.full((LAG,), -1, jnp.int32)], 0)
    paired_all = (segment_ids == segment_next).astype(jnp.int32)
    pair_count = jnp.sum(paired_all.astype(jnp.float32))
    contract = (((0,), (0,)), ((), ()))
    all_frames = jnp.float32(frame_count * n_slab)
    every_rows = lax.all_gather(left_block, "slab", axis=0, tiled=True)
    own_columns = right_block.reshape(frame_count, n_row, n_part, part_width)
    every_columns = lax.all_to_all(own_columns, "slab", split_axis=2, concat_axis=0, tiled=True)
    total_frames = every_columns.shape[0]
    every_columns = every_columns.reshape(total_frames, n_row * part_width)
    lagged_columns = jnp.concatenate(
        [every_columns[LAG:], jnp.zeros((LAG, n_row * part_width), jnp.bfloat16)], 0
    )
    weighted_rows = every_rows * paired_all.astype(jnp.bfloat16)[:, None]
    tile_shape = (tile_height, n_row, 1, part_width)
    instant_sum = lax.dot_general(
        every_rows, every_columns, contract, preferred_element_type=jnp.float32
    ).reshape(tile_shape)
    lagged_sum = lax.dot_general(
        weighted_rows, lagged_columns, contract, preferred_element_type=jnp.float32
    ).reshape(tile_shape)
    return (instant_sum / all_frames, lagged_sum / pair_count)


def solution(mesh):
    placed = (
        P(("slab", "row", "col"), None),
        P(None, None, None, "col"),
        P(None, None, "col"),
        P(),
    )
    return jax.shard_map(
        per_device,
        mesh=mesh,
        in_specs=placed,
        out_specs=(P("row", None, "slab", "col"), P("row", None, "slab", "col")),
        check_vma=False,
    )
```

profile of v0, /device:TPU:0, one launch (start us, length us, event | category | flops | bytes accessed | tf_op | source)
XLA Modules:
  0.0 317.1 jit_solution(8528654247363517120)
XLA Ops:
  7.2 0.7 all-gather.5.cloned.1.call-update
  8.0 14.3 %reshape.46 = bf16[4096,1024]{1,0:T(8,128)(2,1)} reshape(bf16[4096,4,2,128]{3,2,1,0:T(2,128)(2,1)} %param.5) | data formatting | bytes 16777216 | tf_op jit(solution)/shard_map/reshape | solution.py:18
  22.2 33.0 %all-gather.5.cloned.1.call-done = bf16[128,4096]{1,0:T(8,128)(2,1)} async-done(((bf16[8,4096]{1,0:T(8,128)(2,1)}), bf16[128,4096]{1,0:T(8,128)(2,1)}) %all-gather.5.cloned.1.call-update) | async-done | bytes 1048592 | tf_op jit(solution)/shard_map/all_gather | solution.py:17
  55.2 7.3 %fusion.10 = bf16[128,1024]{1,0:T(8,128)(2,1)} fusion(bf16[128,4096]{1,0:T(8,128)(2,1)} %all-gather.5.cloned.1.call-done, bf16[4096,1024]{1,0:T(8,128)(2,1)} %reshape.46, f32[1024]{0:T(1024)S(1)} %bitcast.37), kind=kOutput, calls=%fused_computation.9 | convolution fusion | flops 1074003968 | bytes 9703424 | tf_op jit(solution)/shard_map/dot_general | solution.py:19
  62.6 0.0 all-gather.9.cloned.1.call-start
  62.6 20.1 %all-gather.7.cloned.1.call-done = bf16[512,1024]{1,0:T(8,128)(2,1)} async-done(((bf16[128,1024]{1,0:T(8,128)(2,1)}), bf16[512,1024]{1,0:T(8,128)(2,1)}) %all-gather.7.cloned.1.call-update) | async-done | bytes 1048592 | tf_op jit(solution)/shard_map/all_gather | solution.py:23
  82.8 1.5 copy.13
  84.3 0.7 constant_dynamic-slice_fusion
  85.0 0.0 all-gather.11.cloned.1.call-start
  85.1 52.9 %all-gather.9.cloned.1.call-done = bf16[512,2,2048]{0,2,1:T(8,128)(2,1)} async-done(((bf16[512,2,128]{0,2,1:T(8,128)(2,1)}), bf16[512,2,2048]{0,2,1:T(8,128)(2,1)}) %all-gather.9.cloned.1.call-update) | async-done | bytes 4194320 | tf_op jit(solution)/shard_map/all_gather | solution.py:28
  138.0 1.8 reshape.50
  139.8 1.2 copy.9
  141.1 4.4 %all-to-all-start = ((bf16[512,4,2,128]{3,1,0,2:T(4,128)(2,1)}), bf16[512,4,2,128]{3,1,0,2:T(4,128)(2,1)S(1)}, u32[]{:S(2)}, u32[]{:S(2)}) async-start(bf16[512,4,2,128]{3,1,0,2:T(4,128)(2,1)} %copy.9), calls=%async_computation | async-start | bytes 2097152 | tf_op jit(solution)/shard_map/all_to_all | solution.py:38
  145.5 0.1 slice.6
  145.6 0.6 fusion.12
  146.2 19.0 %all-to-all-done = bf16[512,4,2,128]{3,1,0,2:T(4,128)(2,1)S(1)} async-done(((bf16[512,4,2,128]{3,1,0,2:T(4,128)(2,1)}), bf16[512,4,2,128]{3,1,0,2:T(4,128)(2,1)S(1)}, u32[]{:S(2)}, u32[]{:S(2)}) %all-to-all-start) | async-done | bytes 1048608 | tf_op jit(solution)/shard_map/all_to_all | solution.py:38
  165.2 0.2 copy.18
  165.4 0.2 slice.8
  165.6 0.5 copy.10
  166.2 84.6 %all-gather.11.cloned.1.call-done = bf16[1024,4096]{0,1:T(8,128)(2,1)} async-done(((bf16[512,4096]{0,1:T(8,128)(2,1)}), bf16[1024,4096]{0,1:T(8,128)(2,1)}) %all-gather.11.cloned.1.call-update) | async-done | bytes 8388624 | tf_op jit(solution)/shard_map/all_gather | solution.py:36
  250.7 10.9 %broadcast_divide_fusion = f32[4096,512]{0,1:T(8,128)} fusion(f32[]{:T(128)} %fusion.12, bf16[1024,4096]{0,1:T(8,128)(2,1)} %all-gather.11.cloned.1.call-done, bf16[1024]{0:T(1024)(128)(2,1)S(1)} %get-tuple-element.6, bf16[974,512]{1,0:T(8,128)(2,1)S(1)} %slice.8), kind=kOutput, calls=%fused_computation.5 | convolution fusion | flops 4301258752 | bytes 17776644 | tf_op jit(solution)/shard_map/dot_general | solution.py:49
  261.6 19.0 %copy.12 = f32[4096,4,1,128]{3,2,1,0:T(1,128)} copy(f32[4096,4,1,128]{0,3,1,2:T(8,128)} %bitcast.31) | data formatting | bytes 16777216
  280.6 7.2 %multiply_bitcast_fusion = f32[4096,4,1,128]{3,0,1,2:T(8,128)S(1)} fusion(bf16[4,128,1024]{2,1,0:T(8,128)(2,1)S(1)} %bitcast.36, bf16[1024,4096]{0,1:T(8,128)(2,1)} %all-gather.11.cloned.1.call-done), kind=kOutput, calls=%fused_computation.4 | convolution fusion | flops 4297064448 | bytes 17825792 | tf_op jit(solution)/shard_map/dot_general | solution.py:46
  287.8 22.8 %copy.11 = f32[4096,4,1,128]{3,2,1,0:T(1,128)} copy(f32[4096,4,1,128]{3,0,1,2:T(8,128)S(1)} %multiply_bitcast_fusion) | data formatting | bytes 16777216
  (10 shorter events, 0.1 us)
Async XLA Ops:
  7.2 48.0 %all-gather.5.cloned.1.call-start = ((), (), s32[]{:S(2)}) async-start(), calls=%async_computation.1 | async-start | bytes 1114112 | tf_op jit(solution)/shard_map/all_gather | solution.py:17
  7.9 47.3 %copy-start.1 = (f32[4,2,128]{2,1,0:T(2,128)S(1)}, f32[4,2,128]{2,1,0:T(2,128)}, u32[]{:S(2)}) copy-start(f32[4,2,128]{2,1,0:T(2,128)} %param.6) | copy-start | bytes 12292
  7.9 74.8 %all-gather.7.cloned.1.call-start = ((), (), s32[]{:S(2)}) async-start(), calls=%async_computation.2 | async-start | bytes 1310720 | tf_op jit(solution)/shard_map/all_gather | solution.py:23
  62.5 82.9 %copy-start = (s32[1024]{0:T(1024)S(1)}, s32[1024]{0:T(1024)}, u32[]{:S(2)}) copy-start(s32[1024]{0:T(1024)} %param.7) | copy-start | bytes 12292
  62.6 75.4 %all-gather.9.cloned.1.call-start = ((), (), s32[]{:S(2)}) async-start(), calls=%async_computation.3 | async-start | bytes 4456448 | tf_op jit(solution)/shard_map/all_gather | solution.py:28
  85.0 165.7 %all-gather.11.cloned.1.call-start = ((), (), s32[]{:S(2)}) async-start(), calls=%async_computation.4 | async-start | bytes 12582912 | tf_op jit(solution)/shard_map/all_gather | solution.py:36
  141.1 24.1 %all-to-all-start = ((bf16[512,4,2,128]{3,1,0,2:T(4,128)(2,1)}), bf16[512,4,2,128]{3,1,0,2:T(4,128)(2,1)S(1)}, u32[]{:S(2)}, u32[]{:S(2)}) async-start(bf16[512,4,2,128]{3,1,0,2:T(4,128)(2,1)} %copy.9), calls=%async_computation | async-start | bytes 2097152 | tf_op jit(solution)/shard_map/all_to_all | solution.py:38
Sparse Core Ops, SparseCore 0:
  10.1 45.0 all-gather.4
  62.7 20.0 all-gather.6
  85.5 52.4 all-gather.8
  139.5 111.1 all-gather.10
where the time goes:
time: 319 us; the launch traced here: 317 us
  waiting for transfers between devices  210 us (66%)
  local copies, waits for them, and re-layouts  62.3 us (20%)
  matrix products  25.4 us (8%)
  between operations  13.8 us (4%)
  starting transfers between devices  4.58 us (1%)
    all_gather x1, waiting for transfers between devices, per_device(): every_rows = lax.all_gather(left_block, 'slab', axis=0, tiled=True)  84.6 us
    all_gather x1, waiting for transfers between devices, per_device(): left_block = lax.all_gather(own_rows, 'col', axis=2, tiled=True)  52.9 us
    unnamed x7, local copies, waits for them, and re-layouts  42 us
    all_gather x1, waiting for transfers between devices, per_device(): frame_rows = lax.all_gather(distances, 'col', axis=0, tiled=True)  33 us
    all_gather x1, waiting for transfers between devices, per_device(): right_block = lax.all_gather(own_features, 'row', axis=0, tiled=True)  20.1 us
    all_to_all x1, waiting for transfers between devices, per_device(): lax.all_to_all(own_columns, 'slab', split_axis=2, concat_axis=0, tiled=True)  19 us
    reshape x1, local copies, waits for them, and re-layouts, per_device(): flat_projection = projection.reshape(input_width, local_width)  14.3 us
    dot_general x1, matrix products, per_device(): lax.dot_general(weighted_rows, lagged_columns, contract, preferred_elemen...  10.9 us
  transfers between devices with their start and end apart: 5, of which 5 were waited for; matrix products, arithmetic and copies ran while one was open for 6% of the time, Pallas kernels for 0%

commit v1 on v0

v1 whole, which is shorter than its diff:
```python
import functools

import jax
import jax.numpy as jnp
from jax import lax
from jax.experimental import pallas as pl
from jax.experimental.pallas import tpu as pltpu
from jax.sharding import PartitionSpec as P

LAG = 50
MESH = pl.DeviceIdType.MESH
MIB = 1 << 20
PI_A, PI_B, PI_C = 3.140625, 0.0009670257568359375, 6.2771141529083252e-07
COS_POLY = (
    2.08767570e-09, -2.75573192e-07, 2.48015873e-05, -1.38888889e-03, 4.16666667e-02, -0.5, 1.0
)


def cosine(angle):
    k = jnp.floor(angle * (1.0 / 3.14159265358979) + 0.5)
    r = ((angle - k * PI_A) - k * PI_B) - k * PI_C
    odd = k - 2.0 * jnp.floor(k * 0.5)
    square = r * r
    value = jnp.full_like(square, COS_POLY[0])
    for term in COS_POLY[1:]:
        value = value * square + term
    return value * (1.0 - 2.0 * odd)


def positions():
    slab, row, col = lax.axis_index("slab"), lax.axis_index("row"), lax.axis_index("col")
    return col // 4, col % 4, slab * 2 + row // 2, row % 2


def device(x, y, z, k):
    x, y, z, k = x % 4, y % 4, z % 4, k % 2
    return (z // 2, (z % 2) * 2 + k, x * 4 + y)


def remote(src, dst, send, recv, target):
    return pltpu.make_async_remote_copy(
        src_ref=src, dst_ref=dst, send_sem=send, recv_sem=recv, device_id=target, device_id_type=MESH
    )


def gather_kernel(
    d_ref, p_ref, phase_ref, left_ref, right_ref,
    stage, planes, d_all, d_rows, natural, turned,
    p_sem, d_send, d_recv, l_send, l_recv, r_send, r_recv, g_send, g_recv, own_sem,
):
    x, y, z, k = positions()
    me = z * 2 + k
    n_chunk = 8
    chunk = p_ref.shape[0] // n_chunk

    def p_copy(n):
        rows = pl.ds(n * chunk, chunk)
        return pltpu.make_async_copy(p_ref.at[rows], stage.at[rows], p_sem.at[n])

    for n in range(n_chunk):
        p_copy(n).start()

    for h in range(2):
        low = d_ref[:, h * 1024:(h + 1) * 1024].astype(jnp.float32)
        high = d_ref[:, 2048 + h * 1024:2048 + (h + 1) * 1024].astype(jnp.float32)
        d_all[h, x, y] = jnp.concatenate([low, high], 0).astype(jnp.bfloat16)

    hops = (1, 3, 2)
    along_x = [device(x + d, y, z, k) for d in hops]
    along_y = [device(x, y + d, z, k) for d in hops]
    mates = [(0, 1), (1, 0), (1, 1), (3, 0), (3, 1), (2, 0), (2, 1)]
    barrier = pltpu.get_barrier_semaphore()
    partners = along_x + along_y + [device(x, y, z + dz, k + dk) for dz, dk in mates]
    for partner in partners:
        pl.semaphore_signal(barrier, inc=1, device_id=partner, device_id_type=MESH)
    pl.semaphore_wait(barrier, len(partners))

    first = []
    for i in range(3):
        own = d_all.at[0, x, y]
        first.append(remote(own, own, d_send.at[0, i], d_recv.at[0, i], along_x[i]))
        own = d_all.at[1, x, y]
        first.append(remote(own, own, d_send.at[1, i], d_recv.at[1, i], along_y[i]))
    for copy in first:
        copy.start()

    to = lax.broadcasted_iota(jnp.int32, (256, 256), 0)
    source = lax.broadcasted_iota(jnp.int32, (256, 256), 1)
    permute = jnp.where((to % 32) * 8 + to // 32 == source, 1.0, 0.0).astype(jnp.bfloat16)

    def sort_rows(n, _):
        rows = stage[pl.ds(pl.multiple_of(n * 1024, 1024), 1024), :]
        wide = jnp.concatenate([rows[q * 256:(q + 1) * 256] for q in range(4)], 1)
        out = jnp.dot(permute, wide, preferred_element_type=jnp.float32).astype(jnp.bfloat16)
        for a in range(4):
            for b in range(2):
                part = out[(a * 2 + b) * 32:(a * 2 + b + 1) * 32]
                for q in range(4):
                    at = pl.ds(pl.multiple_of(n * 128 + q * 32, 32), 32)
                    planes[a, at, b * 128:(b + 1) * 128] = part[:, q * 128:(q + 1) * 128]
        return 0

    for n in range(3):
        p_copy(n).wait()
    lax.fori_loop(0, 12, sort_rows, 0)

    for copy in first:
        copy.wait_recv()
    second = []
    for i in range(3):
        line = d_all.at[0, :, y]
        second.append(remote(line, line, d_send.at[0, 3 + i], d_recv.at[0, 3 + i], along_y[i]))
        line = d_all.at[1, x]
        second.append(remote(line, line, d_send.at[1, 3 + i], d_recv.at[1, 3 + i], along_x[i]))
    for copy in second:
        copy.start()
    for n in range(3, n_chunk):
        p_copy(n).wait()
    lax.fori_loop(12, 32, sort_rows, 0)
    for copy in second:
        copy.wait_recv()

    for h in range(2):
        for q in range(2):
            part = d_all[h].astype(jnp.float32).reshape(16, 16, 1024)[:, q * 8:(q + 1) * 8, :]
            at = q * 2048 + h * 1024
            d_rows[:, at:at + 1024] = part.reshape(128, 1024).astype(jnp.bfloat16)

    def features(step, _):
        a = (z % 2 * 2 + k + step) % 4
        angles = jnp.dot(d_rows[...], planes[a], preferred_element_type=jnp.float32)
        shift = phase_ref[pl.ds(a, 1)].reshape(2, 128)
        for b in range(2):
            value = cosine(angles[:, b * 128:(b + 1) * 128] + shift[b:b + 1])
            natural[b, a] = value.astype(jnp.bfloat16)
            turned[a, b] = value.T.astype(jnp.bfloat16)
        return 0

    lax.fori_loop(0, 4, features, 0)

    own_left = pltpu.make_async_copy(turned.at[z % 2 * 2 + k], left_ref.at[me, :, x, y], own_sem.at[0])
    own_right = pltpu.make_async_copy(natural.at[z // 2], right_ref.at[me], own_sem.at[1])
    own_left.start()
    own_right.start()
    lefts, rights = [], []
    for i, (dz, dk) in enumerate(mates):
        z2, k2 = (z + dz) % 4, (k + dk) % 2
        target = device(x, y, z2, k2)
        j = mates.index((-dz % 4, dk))
        lefts.append(remote(
            turned.at[z2 % 2 * 2 + k2], left_ref.at[me, :, x, y], l_send.at[i], l_recv.at[j], target))
        rights.append(remote(natural.at[z2 // 2], right_ref.at[me], r_send.at[i], r_recv.at[j], target))
    for copy in lefts + rights:
        copy.start()
    own_left.wait()

    def slot(step):
        e = step // 2
        dz = e + e // 2 - 2 * (e // 3)
        return (z + dz) % 4 * 2 + (k + step) % 2

    px, mx, py, my = along_x[0], along_x[1], along_y[0], along_y[1]
    xp, xm, yp, ym = (x + 1) % 4, (x + 3) % 4, (y + 1) % 4, (y + 3) % 4

    def copies(group, number):
        g = slot(group)
        half0, half1 = left_ref.at[g, 0], left_ref.at[g, 1]
        low, high = pl.ds(0, 64), pl.ds(64, 64)
        if number == 0:
            pairs = [(half0.at[x, y], px), (half0.at[x, y], mx), (half1.at[x, y], py), (half1.at[x, y], my)]
        elif number == 1:
            pairs = [(half0.at[xm, y, low], px), (half0.at[xp, y, high], mx),
                     (half1.at[x, ym, low], py), (half1.at[x, yp, high], my)]
        elif number == 2:
            pairs = [(half0.at[:, y], py), (half0.at[:, y], my), (half1.at[x], px), (half1.at[x], mx)]
        else:
            pairs = [(half0.at[pl.ds(0, 2), ym], py), (half0.at[pl.ds(2, 2), yp], my),
                     (half1.at[xm, pl.ds(0, 2)], px), (half1.at[xp, pl.ds(2, 2)], mx)]
        return [
            remote(ref, ref, g_send.at[group, number, i], g_recv.at[group, number, i], target)
            for i, (ref, target) in enumerate(pairs)
        ]

    def rounds(step, _):
        for number in range(5):
            group = step - number

            @pl.when(jnp.logical_and(group >= 0, group < 8))
            def _():
                if number > 0:
                    for copy in copies(group, number - 1):
                        copy.wait_recv()
                if number < 4:
                    if number == 0:
                        @pl.when(group > 0)
                        def _():
                            at = left_ref.at[me, :, x, y]
                            i = group - 1
                            remote(at, at, l_send.at[i], l_recv.at[i], px).wait_recv()
                    for copy in copies(group, number):
                        copy.start()
        return 0

    lax.fori_loop(0, 12, rounds, 0)

    own_right.wait()
    for copy in rights:
        copy.wait()
    for copy in lefts + first + second:
        copy.wait_send()

    def drain(group, _):
        for number in range(4):
            for copy in copies(group, number):
                copy.wait_send()
        return 0

    lax.fori_loop(0, 8, drain, 0)


def gather(distances, projection, phases):
    bf16 = jnp.bfloat16
    dma = pltpu.SemaphoreType.DMA
    return pl.pallas_call(
        gather_kernel,
        out_shape=(
            pltpu.VMEM((8, 2, 4, 4, 128, 128), bf16),
            pltpu.VMEM((8, 4, 128, 128), bf16),
        ),
        in_specs=[
            pl.BlockSpec(memory_space=pltpu.VMEM),
            pl.BlockSpec(memory_space=pl.ANY),
            pl.BlockSpec(memory_space=pltpu.VMEM),
        ],
        out_specs=(pl.BlockSpec(memory_space=pltpu.VMEM), pl.BlockSpec(memory_space=pltpu.VMEM)),
        scratch_shapes=[
            pltpu.VMEM((32768, 128), bf16),
            pltpu.VMEM((4, 4096, 256), bf16),
            pltpu.VMEM((2, 4, 4, 16, 1024), bf16),
            pltpu.VMEM((128, 4096), bf16),
            pltpu.VMEM((2, 4, 128, 128), bf16),
            pltpu.VMEM((4, 2, 128, 128), bf16),
            dma((8,)),
            dma((2, 6)),
            dma((2, 6)),
            dma((7,)),
            dma((7,)),
            dma((7,)),
            dma((7,)),
            dma((8, 4, 4)),
            dma((8, 4, 4)),
            dma((2,)),
        ],
        compiler_params=pltpu.CompilerParams(
            collective_id=0, has_side_effects=True, vmem_limit_bytes=44 * MIB
        ),
        name="gather_features",
    )(distances, projection, phases)


def covariance_kernel(left_ref, right_ref, segment_ref, instant_ref, lagged_ref, columns, scale):
    bf16, f32 = jnp.bfloat16, jnp.float32

    @pl.when(pl.program_id(0) == 0)
    def _():
        for g in range(8):
            for a in range(4):
                columns[g * 128:(g + 1) * 128, a * 128:(a + 1) * 128] = right_ref[g, a]
        ids = jnp.broadcast_to(segment_ref[...], (8, 1024))
        frame = lax.broadcasted_iota(jnp.int32, (8, 1024), 1)
        paired = jnp.where((pltpu.roll(ids, LAG, 1) == ids) & (frame >= LAG), 1.0, 0.0).astype(f32)
        scale[0] = 1.0 / jnp.sum(paired[0:1])
        for n in range(8):
            start = min(n * 128, 768)
            here = lax.broadcasted_iota(jnp.int32, (128, 256), 0) + n * 128
            there = lax.broadcasted_iota(jnp.int32, (128, 256), 1) + start
            take = jnp.where(there == here + LAG, paired[0:1, start:start + 256], 0.0).astype(bf16)
            moved = jnp.dot(take, columns[start:start + 256, 0:512], preferred_element_type=f32)
            columns[n * 128:(n + 1) * 128, 512:1024] = moved.astype(bf16)

    rows = jnp.concatenate(
        [jnp.concatenate([left_ref[g, 0, 0, i] for g in range(8)], 1) for i in range(4)], 0
    )
    inverse = scale[0]
    for out_ref, at, factor in ((instant_ref, 0, 1.0 / 1024), (lagged_ref, 512, inverse)):
        total = jnp.dot(rows, columns[:, at:at + 512], preferred_element_type=f32) * factor
        for a in range(4):
            out_ref[pl.ds(a, 512, stride=4), :] = total[:, a * 128:(a + 1) * 128]


def covariances(left, right, segment_ids):
    out = jax.ShapeDtypeStruct((16384, 128), jnp.float32)
    return pl.pallas_call(
        covariance_kernel,
        grid=(8,),
        out_shape=(out, out),
        in_specs=[
            pl.BlockSpec((8, 1, 1, 4, 128, 128), lambda m: (0, m // 4, m % 4, 0, 0, 0)),
            pl.BlockSpec((8, 4, 128, 128), lambda m: (0, 0, 0, 0)),
            pl.BlockSpec((1, 1024), lambda m: (0, 0)),
        ],
        out_specs=(pl.BlockSpec((2048, 128), lambda m: (m, 0)), pl.BlockSpec((2048, 128), lambda m: (m, 0))),
        scratch_shapes=[pltpu.VMEM((1024, 1024), jnp.bfloat16), pltpu.SMEM((1,), jnp.float32)],
        compiler_params=pltpu.CompilerParams(vmem_limit_bytes=40 * MIB),
        name="covariances",
    )(left, right, segment_ids)


def per_device(distances, projection, phases, segment_ids):
    left, right = gather(distances, projection.reshape(32768, 128), phases)
    instant, lagged = covariances(left, right, segment_ids.reshape(1, 1024))
    return instant.reshape(4096, 4, 1, 128), lagged.reshape(4096, 4, 1, 128)


def solution(mesh):
    placed = (
        P(("slab", "row", "col"), None),
        P(None, None, None, "col"),
        P(None, None, "col"),
        P(),
    )
    return jax.shard_map(
        per_device,
        mesh=mesh,
        in_specs=placed,
        out_specs=(P("row", None, "slab", "col"), P("row", None, "slab", "col")),
        check_vma=False,
    )
```

time: 319 us -> 89.2 us (0.28)
  waiting for transfers between devices: 210 us -> 0 us
  Pallas kernels: 0 us -> 86.9 us
  local copies, waits for them, and re-layouts: 62.3 us -> 1.52 us
  matrix products: 25.4 us -> 0 us
  between operations: 13.8 us -> 0.66 us
  starting transfers between devices: 4.58 us -> 0 us
    all_gather x4 -> x0, waiting for transfers between devices: 191 us -> none  [the longest x1 84.6 us: per_device(): every_rows = lax.all_gather(left_block, 'slab', axis=0, tiled=True)]
    pallas_call x0 -> x2, Pallas kernels: none -> 86.9 us  [the longest x1 74.2 us: gather(): pl.pallas_call(gather_kernel, out_shape=(pltpu.VMEM((8, 2, 4, 4, 128, 128...]
    unnamed x7 -> x6, local copies, waits for them, and re-layouts: 42 us -> 1.52 us
    dot_general x3 -> x0, matrix products: 25.4 us -> none  [the longest x1 10.9 us: per_device(): lax.dot_general(weighted_rows, lagged_columns, contract, preferred_elemen...]
    all_to_all x1 -> x0, waiting for transfers between devices: 19 us -> none  [per_device(): lax.all_to_all(own_columns, 'slab', split_axis=2, concat_axis=0, tiled=True)]
    reshape x4 -> x0, local copies, waits for them, and re-layouts: 18.8 us -> none  [the longest x1 14.3 us: per_device(): flat_projection = projection.reshape(input_width, local_width)]
    all_to_all x1 -> x0, starting transfers between devices: 4.42 us -> none  [per_device(): lax.all_to_all(own_columns, 'slab', split_axis=2, concat_axis=0, tiled=True)]
  transfers between devices with their start and end apart: 5 -> 0, of which waited for: 5 -> 0; matrix products, arithmetic and copies ran while one was open for 6% -> 0% of each run, Pallas kernels for 0% -> 0%
where the time goes in v1:
time: 89.2 us; the launch traced here: 89 us
  Pallas kernels  86.9 us (97%)
  local copies, waits for them, and re-layouts  1.52 us (2%)
    pallas_call x1, Pallas kernels, gather(): pl.pallas_call(gather_kernel, out_shape=(pltpu.VMEM((8, 2, 4, 4, 128, 128...  74.2 us
    pallas_call x1, Pallas kernels, covariances(): pl.pallas_call(covariance_kernel, grid=(8,), out_shape=(out, out), in_spe...  12.7 us

profile of v1, /device:TPU:0, one launch (start us, length us, event | category | flops | bytes accessed | tf_op | source)
XLA Modules:
  0.0 89.0 jit_solution(18123270444241400329)
XLA Ops:
  0.6 0.0 copy-start
  0.6 0.8 copy-done
  1.5 0.0 copy-start.1
  1.5 0.7 copy-done.1
  2.2 0.0 copy-start.2
  2.2 74.2 %gather_features.1 = (bf16[8,2,4,4,128,128]{5,4,3,2,1,0:T(8,128)(2,1)S(1)}, bf16[8,4,128,128]{3,2,1,0:T(8,128)(2,1)S(1)}) custom-call(bf16[8,4096]{1,0:T(8,128)(2,1)S(1)} %copy-done, bf16[32768,128]{1,0:T(8,128)(2,1)} %bitcast.9, f32[4,2,128]{2,1,0:T(2,128)S(1)} %copy-done.1), custom_call_target="tpu_custom_call" | custom-call | tf_op jit(solution)/shard_map/gather_features/pallas_call | solution.py:224
  76.3 0.0 copy-done.2
  76.4 12.7 %covariances.1 = (f32[16384,128]{1,0:T(8,128)}, f32[16384,128]{1,0:T(8,128)}) custom-call(bf16[8,2,4,4,128,128]{5,4,3,2,1,0:T(8,128)(2,1)S(1)} %get-tuple-element.6.left_ref, bf16[8,4,128,128]{3,2,1,0:T(8,128)(2,1)S(1)} %get-tuple-element.7.right_ref, s32[1,1024]{1,0:T(1,128)S(1)} %bitcast.8), custom_call_target="tpu_custom_call" | custom-call | tf_op jit(solution)/shard_map/covariances/pallas_call | solution.py:293
Async XLA Ops:
  0.6 0.8 copy-start
  1.5 0.7 copy-start.1
  2.2 74.2 %copy-start.2 = (s32[1024]{0:T(1024)S(1)}, s32[1024]{0:T(1024)}, u32[]{:S(2)}) copy-start(s32[1024]{0:T(1024)} %param.7) | copy-start | bytes 12292

commit v2 on v1

v2 whole, which is shorter than its diff:
```python
import functools

import jax
import jax.numpy as jnp
from jax import lax
from jax.experimental import pallas as pl
from jax.experimental.pallas import tpu as pltpu
from jax.sharding import PartitionSpec as P

LAG = 50
MESH = pl.DeviceIdType.MESH
MIB = 1 << 20
PI_A, PI_B, PI_C = 3.140625, 0.0009670257568359375, 6.2771141529083252e-07
COS_POLY = (
    2.08767570e-09, -2.75573192e-07, 2.48015873e-05, -1.38888889e-03, 4.16666667e-02, -0.5, 1.0
)


def cosine(angle):
    k = jnp.floor(angle * (1.0 / 3.14159265358979) + 0.5)
    r = ((angle - k * PI_A) - k * PI_B) - k * PI_C
    odd = k - 2.0 * jnp.floor(k * 0.5)
    square = r * r
    value = jnp.full_like(square, COS_POLY[0])
    for term in COS_POLY[1:]:
        value = value * square + term
    return value * (1.0 - 2.0 * odd)


def positions():
    slab, row, col = lax.axis_index("slab"), lax.axis_index("row"), lax.axis_index("col")
    return col // 4, col % 4, slab * 2 + row // 2, row % 2


def device(x, y, z, k):
    x, y, z, k = x % 4, y % 4, z % 4, k % 2
    return (z // 2, (z % 2) * 2 + k, x * 4 + y)


def remote(src, dst, send, recv, target):
    return pltpu.make_async_remote_copy(
        src_ref=src, dst_ref=dst, send_sem=send, recv_sem=recv, device_id=target, device_id_type=MESH
    )


def gather_kernel(
    d_hbm, p_ref, phase_hbm, segment_hbm, instant_ref, lagged_ref, left_ref, columns,
    d_ref, phase_ref, segment_ref, stage, planes, d_all, d_rows, partial, natural, turned, right_ref, scale,
    in_sem, p_sem, d_send, d_recv, e_send, e_recv, r_send, r_recv, g_send, g_recv, x_send, x_recv, own_sem,
):
    x, y, z, k = positions()
    me, slab, row = z * 2 + k, z // 2, z % 2 * 2 + k
    n_chunk = 8
    chunk = p_ref.shape[0] // n_chunk

    def p_copy(n):
        rows = pl.ds(n * chunk, chunk)
        return pltpu.make_async_copy(p_ref.at[rows], stage.at[rows], p_sem.at[n])

    d_copy = pltpu.make_async_copy(d_hbm, d_ref, in_sem.at[0])
    phase_copy = pltpu.make_async_copy(phase_hbm, phase_ref, in_sem.at[1])
    segment_copy = pltpu.make_async_copy(segment_hbm, segment_ref, in_sem.at[2])
    d_copy.start()
    phase_copy.start()
    segment_copy.start()
    for n in range(n_chunk):
        p_copy(n).start()

    hops = (1, 3, 2)
    along_x = [device(x + d, y, z, k) for d in hops]
    along_y = [device(x, y + d, z, k) for d in hops]
    mates = [(0, 1), (1, 0), (1, 1), (3, 0), (3, 1), (2, 0), (2, 1)]
    barrier = pltpu.get_barrier_semaphore()
    partners = along_x + along_y + [device(x, y, z + dz, k + dk) for dz, dk in mates]
    for partner in partners:
        pl.semaphore_signal(barrier, inc=1, device_id=partner, device_id_type=MESH)

    d_copy.wait()
    for h in range(2):
        for e in range(2):
            at = h * 1024 + e * 512
            low = d_ref[:, at:at + 512].astype(jnp.float32)
            high = d_ref[:, 2048 + at:2048 + at + 512].astype(jnp.float32)
            d_all[h, e, x, y] = jnp.concatenate([low, high], 0).astype(jnp.bfloat16)
    pl.semaphore_wait(barrier, len(partners))

    first = []
    for i in range(3):
        own = d_all.at[0, :, x, y]
        first.append(remote(own, own, d_send.at[0, i], d_recv.at[0, i], along_x[i]))
        own = d_all.at[1, :, x, y]
        first.append(remote(own, own, d_send.at[1, i], d_recv.at[1, i], along_y[i]))
    for copy in first:
        copy.start()

    to = lax.broadcasted_iota(jnp.int32, (256, 256), 0)
    source = lax.broadcasted_iota(jnp.int32, (256, 256), 1)
    permute = jnp.where((to % 32) * 8 + to // 32 == source, 1.0, 0.0).astype(jnp.bfloat16)

    def sort_rows(n, _):
        part = n // 4
        place = part % 2 * 2048 + part // 2 * 512 + n % 4 * 128
        rows = stage[pl.ds(pl.multiple_of(n * 1024, 1024), 1024), :]
        wide = jnp.concatenate([rows[q * 256:(q + 1) * 256] for q in range(4)], 1)
        out = jnp.dot(permute, wide, preferred_element_type=jnp.float32).astype(jnp.bfloat16)
        for a in range(4):
            for b in range(2):
                part = out[(a * 2 + b) * 32:(a * 2 + b + 1) * 32]
                lanes = slice(a % 2 * 128, a % 2 * 128 + 128)
                for q in range(4):
                    at = pl.ds(pl.multiple_of(place + q * 32, 32), 32)
                    planes[b * 2 + a // 2, at, lanes] = part[:, q * 128:(q + 1) * 128]
        return 0

    for n in range(3):
        p_copy(n).wait()
    lax.fori_loop(0, 12, sort_rows, 0, unroll=4)

    for copy in first:
        copy.wait_recv()
    second = []
    for e in range(2):
        for i in range(3):
            n = 3 + e * 3 + i
            line = d_all.at[0, e, :, y]
            second.append(remote(line, line, d_send.at[0, n], d_recv.at[0, n], along_y[i]))
            line = d_all.at[1, e, x]
            second.append(remote(line, line, d_send.at[1, n], d_recv.at[1, n], along_x[i]))
    for copy in second:
        copy.start()
    for n in range(3, n_chunk):
        p_copy(n).wait()
    lax.fori_loop(12, 32, sort_rows, 0, unroll=4)
    phase_copy.wait()
    segment_copy.wait()

    def arrive(e):
        for copy in second[e * 6:(e + 1) * 6]:
            copy.wait_recv()
        for q in range(2):
            for h in range(2):
                part = d_all[h, e].astype(jnp.float32).reshape(16, 16, 512)[:, q * 8:(q + 1) * 8, :]
                at = e * 2048 + (q * 2 + h) * 512
                d_rows[:, at:at + 512] = part.reshape(128, 512).astype(jnp.bfloat16)

    def product(p, e):
        depth = slice(e * 2048, (e + 1) * 2048)
        return jnp.dot(d_rows[:, depth], planes[p, depth, :], preferred_element_type=jnp.float32)

    arrive(0)
    for p in range(4):
        partial[p] = product(p, 0)
    arrive(1)

    def features(b):
        for p in range(2):
            angles = partial[b * 2 + p] + product(b * 2 + p, 1)
            for i in range(2):
                a = p * 2 + i
                value = cosine(angles[:, i * 128:(i + 1) * 128] + phase_ref[a, b:b + 1])
                natural[b, a] = value.astype(jnp.bfloat16)
                turned[a, b * 4:(b + 1) * 4] = value.T.astype(jnp.bfloat16).reshape(4, 2, 16, 128)

    def frames(ref):
        return ref.at[:, :, x, y, slab, :, pl.ds(pl.multiple_of(row * 128, 128), 128)]

    batches = [(pl.ds(0, 1), None), (pl.ds(1, 2), pl.ds(2, 2)), (pl.ds(3, 4), pl.ds(4, 4))]
    own, shares = [], []
    for n, (slots, chunks) in enumerate(batches):
        mine = pl.ds(slab, 1) if chunks is None else chunks
        own.append(pltpu.make_async_copy(turned.at[row, mine], frames(left_ref.at[slots]), own_sem.at[n]))
        for i, (dz, dk) in enumerate(mates):
            j = mates.index((-dz % 4, dk))
            z2, k2 = (z + dz) % 4, (k + dk) % 2
            theirs = pl.ds(z2 // 2, 1) if chunks is None else chunks
            shares.append(remote(
                turned.at[z2 % 2 * 2 + k2, theirs], frames(left_ref.at[slots]),
                e_send.at[n, i], e_recv.at[n, j], device(x, y, z2, k2)))
    own.append(pltpu.make_async_copy(natural.at[slab], right_ref.at[me], own_sem.at[3]))
    mate = device(x, y, z, k + 1)
    rights = []
    for i, dz in enumerate(hops):
        target = device(x, y, z + dz, k)
        rights.append(remote(
            natural.at[(z + dz) % 4 // 2], right_ref.at[me], r_send.at[i], r_recv.at[hops.index(-dz % 4)], target))
    rights.append(remote(natural.at[slab], right_ref.at[me], r_send.at[3], r_recv.at[3], mate))
    handed = []
    for i, dz in enumerate(hops):
        at = right_ref.at[(z + dz) % 4 * 2 + k]
        handed.append(remote(at, at, r_send.at[4 + i], r_recv.at[4 + i], mate))

    features(0)
    for copy in own[:2] + shares[:14]:
        copy.start()
    features(1)
    for copy in own[2:] + shares[14:] + rights:
        copy.start()
    for copy in own[:3]:
        copy.wait()

    px, mx, py, my = along_x[0], along_x[1], along_y[0], along_y[1]
    xp, xm, yp, ym = (x + 1) % 4, (x + 3) % 4, (y + 1) % 4, (y + 3) % 4

    def copies(slot, number):
        half0, half1 = left_ref.at[slot, 0], left_ref.at[slot, 1]
        if number == 0:
            pairs = [(half0.at[x, y], px), (half0.at[x, y], mx), (half1.at[x, y], py), (half1.at[x, y], my)]
        elif number == 1:
            pairs = [(half0.at[xm, y, 0], px), (half0.at[xp, y, 1], mx),
                     (half1.at[x, ym, 0], py), (half1.at[x, yp, 1], my)]
        elif number == 2:
            pairs = [(half0.at[:, y], py), (half0.at[:, y], my), (half1.at[x], px), (half1.at[x], mx)]
        else:
            pairs = [(half0.at[pl.ds(0, 2), ym], py), (half0.at[pl.ds(2, 2), yp], my),
                     (half1.at[xm, pl.ds(0, 2)], px), (half1.at[xp, pl.ds(2, 2)], mx)]
        return [
            remote(ref, ref, g_send.at[slot, number, i], g_recv.at[slot, number, i], target)
            for i, (ref, target) in enumerate(pairs)
        ]

    def crossing(h):
        return remote(left_ref.at[0, h], left_ref.at[7, h], x_send.at[h], x_recv.at[h], device(x, y, z + 2, k))

    def wait_shares(n):
        for copy in shares[n * 7:(n + 1) * 7]:
            copy.wait_recv()

    def multiply(slot, number):
        b, quarter = number // 4, number % 4
        rows = chunk_rows(left_ref, slot)
        for out_ref, at, factor in ((instant_ref, 0, 1.0 / 1024), (lagged_ref, 512, scale[0])):
            total = jnp.dot(rows, columns[:, at:at + 512], preferred_element_type=jnp.float32) * factor
            for c in range(16):
                for a in range(4):
                    part = total[c * 32:(c + 1) * 32, a * 128:(a + 1) * 128]
                    out_ref[b, c, quarter, pl.ds(a, 32, stride=4), :] = part

    def rounds(step, _):
        for number, lead in ((2, 3), (3, 4), (1, 1), (0, 0), (4, 5)):
            slot = step - lead

            @pl.when(jnp.logical_and(slot >= 0, slot < 7))
            def _():
                if number > 0:
                    for copy in copies(slot, number - 1):
                        copy.wait_recv()
                if number == 0:
                    for n, at in enumerate((0, 1, 3)):
                        pl.when(slot == at)(functools.partial(wait_shares, n))
                if number < 4:
                    for copy in copies(slot, number):
                        copy.start()
                else:
                    @pl.when(slot == 0)
                    def _():
                        for h in range(2):
                            crossing(h).start()

                    for earlier in range(4):
                        for copy in copies(slot, earlier):
                            copy.wait_send()
        return 0

    def job(n, _):
        slot = n + jnp.where(n == 5, 2, 0) - jnp.where(n == 6, 1, 0)

        @pl.when(n == 5)
        def _():
            for h in range(2):
                crossing(h).wait_recv()

        multiply(slot, jnp.where(slot == 7, 1 - slab, jnp.where(slot == 0, slab, slot + 1)))
        return 0

    def later(step, _):
        rounds(step, 0)
        begin = jnp.minimum(2 * (step - 7), 5)
        end = jnp.where(step == 10, 7, jnp.minimum(2 * (step - 6), 5))
        lax.fori_loop(begin, end, job, 0)
        return 0

    lax.fori_loop(0, 6, rounds, 0)
    for copy in rights[:3]:
        copy.wait_recv()
    for copy in handed:
        copy.start()
    lax.fori_loop(6, 7, rounds, 0)
    own[3].wait()
    rights[3].wait_recv()
    for copy in handed:
        copy.wait_recv()
    right_columns(right_ref, segment_ref, columns, scale)
    for copy in first + second + shares + rights + handed:
        copy.wait_send()
    lax.fori_loop(7, 11, later, 0)
    for h in range(2):
        crossing(h).wait_send()
    lax.fori_loop(11, 12, rounds, 0)


def chunk_rows(left_ref, slot):
    return jnp.concatenate(
        [
            jnp.concatenate([left_ref[slot, h, x, y, f] for f in range(2)], 1)
            for x in range(4) for y in range(4) for h in range(2)
        ],
        0,
    )


def paired_before(segment_ref):
    ids = jnp.broadcast_to(segment_ref[...], (8, 1024))
    frame = lax.broadcasted_iota(jnp.int32, (8, 1024), 1)
    return jnp.where((pltpu.roll(ids, LAG, 1) == ids) & (frame >= LAG), 1.0, 0.0)[0:1]


def right_columns(right_ref, segment_ref, columns, scale):
    paired = paired_before(segment_ref)
    scale[0] = 1.0 / jnp.sum(paired)
    for g in range(8):
        for a in range(4):
            columns[g * 128:(g + 1) * 128, a * 128:(a + 1) * 128] = right_ref[g, a]
    for n in range(8):
        start = min(n * 128, 768)
        here = lax.broadcasted_iota(jnp.int32, (128, 256), 0) + n * 128
        there = lax.broadcasted_iota(jnp.int32, (128, 256), 1) + start
        take = jnp.where(there == here + LAG, paired[:, start:start + 256], 0.0).astype(jnp.bfloat16)
        moved = jnp.dot(take, columns[start:start + 256, 0:512], preferred_element_type=jnp.float32)
        columns[n * 128:(n + 1) * 128, 512:1024] = moved.astype(jnp.bfloat16)


TILES = (2, 16, 4, 128, 128)


def gather(distances, projection, phases, segment_ids):
    bf16, f32 = jnp.bfloat16, jnp.float32
    dma = pltpu.SemaphoreType.DMA
    anywhere = pl.BlockSpec(memory_space=pl.ANY)
    vmem = pl.BlockSpec(memory_space=pltpu.VMEM)
    return pl.pallas_call(
        gather_kernel,
        out_shape=(
            pltpu.VMEM(TILES, f32),
            pltpu.VMEM(TILES, f32),
            pltpu.VMEM((8, 2, 4, 4, 2, 16, 512), bf16),
            pltpu.VMEM((1024, 1024), bf16),
        ),
        in_specs=[anywhere] * 4,
        out_specs=(vmem,) * 4,
        scratch_shapes=[
            pltpu.VMEM((8, 4096), bf16),
            pltpu.VMEM((4, 2, 128), f32),
            pltpu.VMEM((1, 1024), jnp.int32),
            pltpu.VMEM((32768, 128), bf16),
            pltpu.VMEM((4, 4096, 256), bf16),
            pltpu.VMEM((2, 2, 4, 4, 16, 512), bf16),
            pltpu.VMEM((128, 4096), bf16),
            pltpu.VMEM((4, 128, 256), f32),
            pltpu.VMEM((2, 4, 128, 128), bf16),
            pltpu.VMEM((4, 8, 2, 16, 128), bf16),
            pltpu.VMEM((8, 4, 128, 128), bf16),
            pltpu.SMEM((1,), f32),
            dma((3,)),
            dma((8,)),
            dma((2, 9)),
            dma((2, 9)),
            dma((3, 7)),
            dma((3, 7)),
            dma((7,)),
            dma((7,)),
            dma((7, 4, 4)),
            dma((7, 4, 4)),
            dma((2,)),
            dma((2,)),
            dma((4,)),
        ],
        compiler_params=pltpu.CompilerParams(
            collective_id=0, has_side_effects=True, vmem_limit_bytes=36 * MIB
        ),
        name="gather_features",
    )(distances, projection, phases, segment_ids)


LAST_SLOT, LAST_CHUNK = 6, 7


def finish_kernel(
    instant_tiles, lagged_tiles, left_ref, columns, segment_ref, instant_ref, lagged_ref, instant_last, lagged_last, sem
):
    copies = []

    def move(source, target, n):
        copy = pltpu.make_async_copy(source, target, sem.at[n])
        copy.start()
        copies.append(copy)

    outs = ((instant_tiles, instant_ref, instant_last), (lagged_tiles, lagged_ref, lagged_last))
    for i, (tiles, out_ref, _) in enumerate(outs):
        move(tiles.at[0], out_ref.at[0], i * 3)
        move(tiles.at[1, :, pl.ds(0, 3)], out_ref.at[1, :, pl.ds(0, 3)], i * 3 + 1)
    rows = chunk_rows(left_ref, LAST_SLOT)
    inverse = 1.0 / jnp.sum(paired_before(segment_ref))
    for i, (_, out_ref, last) in enumerate(outs):
        total = jnp.dot(rows, columns[:, i * 512:(i + 1) * 512], preferred_element_type=jnp.float32)
        total = total * (inverse if i else 1.0 / 1024)
        for c in range(16):
            for a in range(4):
                last[c, pl.ds(a, 32, stride=4), :] = total[c * 32:(c + 1) * 32, a * 128:(a + 1) * 128]
        move(last, out_ref.at[1, :, 3], i * 3 + 2)
    for copy in copies:
        copy.wait()


def finish(tiles, segment_ids):
    out = jax.ShapeDtypeStruct(TILES, jnp.float32)
    vmem = pl.BlockSpec(memory_space=pltpu.VMEM)
    anywhere = pl.BlockSpec(memory_space=pl.ANY)
    return pl.pallas_call(
        finish_kernel,
        out_shape=(out, out),
        in_specs=[vmem] * 5,
        out_specs=(anywhere, anywhere),
        scratch_shapes=[
            pltpu.VMEM((16, 128, 128), jnp.float32),
            pltpu.VMEM((16, 128, 128), jnp.float32),
            pltpu.SemaphoreType.DMA((6,)),
        ],
        compiler_params=pltpu.CompilerParams(vmem_limit_bytes=4 * MIB),
        name="covariances",
    )(*tiles, segment_ids)


def per_device(distances, projection, phases, segment_ids):
    segments = segment_ids.reshape(1, 1024)
    tiles = gather(distances, projection.reshape(32768, 128), phases, segments)
    tiles = [pltpu.with_memory_space_constraint(part, pltpu.VMEM) for part in tiles]
    instant, lagged = finish(tiles, segments)
    return instant.reshape(4096, 4, 1, 128), lagged.reshape(4096, 4, 1, 128)


def solution(mesh):
    placed = (
        P(("slab", "row", "col"), None),
        P(None, None, None, "col"),
        P(None, None, "col"),
        P(),
    )
    return jax.shard_map(
        per_device,
        mesh=mesh,
        in_specs=placed,
        out_specs=(P("row", None, "slab", "col"), P("row", None, "slab", "col")),
        check_vma=False,
    )
```

time: 89.2 us -> 79.8 us (0.89)
  Pallas kernels: 86.9 us -> 79.1 us
  local copies, waits for them, and re-layouts: 1.52 us -> 0.01 us
    pallas_call x2, Pallas kernels: 86.9 us -> 79.1 us  [the longest x1 73.2 us: gather(): pl.pallas_call(gather_kernel, out_shape=(pltpu.VMEM(TILES, f32), pltpu.VM...]
    unnamed x6 -> x2, local copies, waits for them, and re-layouts: 1.52 us -> 0.01 us
where the time goes in v2:
time: 79.8 us; the launch traced here: 79.7 us
  Pallas kernels  79.1 us (99%)
    pallas_call x1, Pallas kernels, gather(): pl.pallas_call(gather_kernel, out_shape=(pltpu.VMEM(TILES, f32), pltpu.VM...  73.2 us
    pallas_call x1, Pallas kernels, finish(): pl.pallas_call(finish_kernel, out_shape=(out, out), in_specs=[vmem] * 5,...  5.87 us

profile of v2, /device:TPU:0, one launch (start us, length us, event | category | flops | bytes accessed | tf_op | source)
XLA Modules:
  0.0 79.7 jit_solution(10865518151414500887)
XLA Ops:
  0.6 0.0 copy-start
  0.6 73.2 %gather_features.1 = (f32[2,16,4,128,128]{4,3,2,1,0:T(8,128)S(1)}, f32[2,16,4,128,128]{4,3,2,1,0:T(8,128)S(1)}, bf16[8,2,4,4,2,16,512]{6,5,4,3,2,1,0:T(8,128)(2,1)S(1)}, bf16[1024,1024]{1,0:T(8,128)(2,1)S(1)}) custom-call(bf16[8,4096]{1,0:T(8,128)(2,1)} %d_hbm.1, bf16[32768,128]{1,0:T(8,128)(2,1)} %bitcast.10, f32[4,2,128]{2,1,0:T(2,128)} %phase_hbm.1, ...), custom_call_target="tpu_custom_call" | custom-call | tf_op jit(solution)/shard_map/gather_features/pallas_call | solution.py:340
  73.8 0.0 copy-done
  73.8 5.9 %covariances.1 = (f32[2,16,4,128,128]{4,3,2,1,0:T(8,128)}, f32[2,16,4,128,128]{4,3,2,1,0:T(8,128)}) custom-call(f32[2,16,4,128,128]{4,3,2,1,0:T(8,128)S(1)} %get-tuple-element.8.instant_tiles, f32[2,16,4,128,128]{4,3,2,1,0:T(8,128)S(1)} %get-tuple-element.9.lagged_tiles, bf16[8,2,4,4,2,16,512]{6,5,4,3,2,1,0:T(8,128)(2,1)S(1)} %get-tuple-element.10.left_ref, ...), custom_call_target="tpu_custom_call" | custom-call | tf_op jit(solution)/shard_map/covariances/pallas_call | solution.py:418
Async XLA Ops:
  0.6 73.2 %copy-start = (s32[1024]{0:T(1024)S(1)}, s32[1024]{0:T(1024)}, u32[]{:S(2)}) copy-start(s32[1024]{0:T(1024)} %param.7) | copy-start | bytes 12292

commit v3 on v2

--- a/solution.py
+++ b/solution.py
@@ -45,7 +45,7 @@
 
 def gather_kernel(
     d_hbm, p_ref, phase_hbm, segment_hbm, instant_ref, lagged_ref, left_ref, columns,
-    d_ref, phase_ref, segment_ref, stage, planes, d_all, d_rows, partial, natural, turned, right_ref, scale,
+    d_ref, phase_ref, segment_ref, stage, planes, d_all, d_rows, natural, turned, right_ref, scale,
     in_sem, p_sem, d_send, d_recv, e_send, e_recv, r_send, r_recv, g_send, g_recv, x_send, x_recv, own_sem,
 ):
     x, y, z, k = positions()
@@ -77,29 +77,34 @@
 
     d_copy.wait()
     for h in range(2):
-        for e in range(2):
-            at = h * 1024 + e * 512
-            low = d_ref[:, at:at + 512].astype(jnp.float32)
-            high = d_ref[:, 2048 + at:2048 + at + 512].astype(jnp.float32)
-            d_all[h, e, x, y] = jnp.concatenate([low, high], 0).astype(jnp.bfloat16)
+        low = d_ref[:, h * 1024:(h + 1) * 1024].astype(jnp.float32)
+        high = d_ref[:, 2048 + h * 1024:2048 + (h + 1) * 1024].astype(jnp.float32)
+        d_all[h, x, y] = jnp.concatenate([low, high], 0).astype(jnp.bfloat16)
     pl.semaphore_wait(barrier, len(partners))
 
-    first = []
-    for i in range(3):
-        own = d_all.at[0, :, x, y]
-        first.append(remote(own, own, d_send.at[0, i], d_recv.at[0, i], along_x[i]))
-        own = d_all.at[1, :, x, y]
-        first.append(remote(own, own, d_send.at[1, i], d_recv.at[1, i], along_y[i]))
-    for copy in first:
-        copy.start()
+    axes = (along_x, along_y)
+
+    def send_block(h, block_x, block_y, line, n):
+        block = d_all.at[h, block_x, block_y]
+        copies = [remote(block, block, d_send.at[h, n + i], d_recv.at[h, n + i], line[i]) for i in range(3)]
+        for copy in copies:
+            copy.start()
+        return copies
+
+    first = [send_block(h, x, y, axes[h], 0) for h in range(2)]
+    second = [copy for h in range(2) for copy in send_block(h, x, y, axes[1 - h], 3)]
+    for i, hop in enumerate(hops):
+        for h in range(2):
+            first[h][i].wait_recv()
+            from_x, from_y = ((x - hop) % 4, y) if h == 0 else (x, (y - hop) % 4)
+            second += send_block(h, from_x, from_y, axes[1 - h], 6 + 3 * i)
+    first = first[0] + first[1]
 
     to = lax.broadcasted_iota(jnp.int32, (256, 256), 0)
     source = lax.broadcasted_iota(jnp.int32, (256, 256), 1)
     permute = jnp.where((to % 32) * 8 + to // 32 == source, 1.0, 0.0).astype(jnp.bfloat16)
 
-    def sort_rows(n, _):
-        part = n // 4
-        place = part % 2 * 2048 + part // 2 * 512 + n % 4 * 128
+    def sort_rows(n):
         rows = stage[pl.ds(pl.multiple_of(n * 1024, 1024), 1024), :]
         wide = jnp.concatenate([rows[q * 256:(q + 1) * 256] for q in range(4)], 1)
         out = jnp.dot(permute, wide, preferred_element_type=jnp.float32).astype(jnp.bfloat16)
@@ -108,75 +113,47 @@
                 part = out[(a * 2 + b) * 32:(a * 2 + b + 1) * 32]
                 lanes = slice(a % 2 * 128, a % 2 * 128 + 128)
                 for q in range(4):
-                    at = pl.ds(pl.multiple_of(place + q * 32, 32), 32)
+                    at = pl.ds(pl.multiple_of(n * 128 + q * 32, 32), 32)
                     planes[b * 2 + a // 2, at, lanes] = part[:, q * 128:(q + 1) * 128]
+
+    def sort_chunk(n, _):
+        p_copy(n).wait()
+        for i in range(4):
+            sort_rows(n * 4 + i)
         return 0
 
-    for n in range(3):
-        p_copy(n).wait()
-    lax.fori_loop(0, 12, sort_rows, 0, unroll=4)
-
-    for copy in first:
-        copy.wait_recv()
-    second = []
-    for e in range(2):
-        for i in range(3):
-            n = 3 + e * 3 + i
-            line = d_all.at[0, e, :, y]
-            second.append(remote(line, line, d_send.at[0, n], d_recv.at[0, n], along_y[i]))
-            line = d_all.at[1, e, x]
-            second.append(remote(line, line, d_send.at[1, n], d_recv.at[1, n], along_x[i]))
-    for copy in second:
-        copy.start()
-    for n in range(3, n_chunk):
-        p_copy(n).wait()
-    lax.fori_loop(12, 32, sort_rows, 0, unroll=4)
+    lax.fori_loop(0, n_chunk, sort_chunk, 0)
     phase_copy.wait()
     segment_copy.wait()
-
-    def arrive(e):
-        for copy in second[e * 6:(e + 1) * 6]:
-            copy.wait_recv()
+    for copy in second:
+        copy.wait_recv()
+    for h in range(2):
         for q in range(2):
-            for h in range(2):
-                part = d_all[h, e].astype(jnp.float32).reshape(16, 16, 512)[:, q * 8:(q + 1) * 8, :]
-                at = e * 2048 + (q * 2 + h) * 512
-                d_rows[:, at:at + 512] = part.reshape(128, 512).astype(jnp.bfloat16)
-
-    def product(p, e):
-        depth = slice(e * 2048, (e + 1) * 2048)
-        return jnp.dot(d_rows[:, depth], planes[p, depth, :], preferred_element_type=jnp.float32)
-
-    arrive(0)
-    for p in range(4):
-        partial[p] = product(p, 0)
-    arrive(1)
+            part = d_all[h].astype(jnp.float32).reshape(16, 16, 1024)[:, q * 8:(q + 1) * 8, :]
+            at = q * 2048 + h * 1024
+            d_rows[:, at:at + 1024] = part.reshape(128, 1024).astype(jnp.bfloat16)
 
     def features(b):
         for p in range(2):
-            angles = partial[b * 2 + p] + product(b * 2 + p, 1)
+            angles = jnp.dot(d_rows[...], planes[b * 2 + p], preferred_element_type=jnp.float32)
             for i in range(2):
                 a = p * 2 + i
                 value = cosine(angles[:, i * 128:(i + 1) * 128] + phase_ref[a, b:b + 1])
                 natural[b, a] = value.astype(jnp.bfloat16)
                 turned[a, b * 4:(b + 1) * 4] = value.T.astype(jnp.bfloat16).reshape(4, 2, 16, 128)
 
-    def frames(ref):
-        return ref.at[:, :, x, y, slab, :, pl.ds(pl.multiple_of(row * 128, 128), 128)]
-
     batches = [(pl.ds(0, 1), None), (pl.ds(1, 2), pl.ds(2, 2)), (pl.ds(3, 4), pl.ds(4, 4))]
-    own, shares = [], []
+    shares = []
     for n, (slots, chunks) in enumerate(batches):
-        mine = pl.ds(slab, 1) if chunks is None else chunks
-        own.append(pltpu.make_async_copy(turned.at[row, mine], frames(left_ref.at[slots]), own_sem.at[n]))
         for i, (dz, dk) in enumerate(mates):
             j = mates.index((-dz % 4, dk))
             z2, k2 = (z + dz) % 4, (k + dk) % 2
             theirs = pl.ds(z2 // 2, 1) if chunks is None else chunks
+            group = (me - (z2 * 2 + k2) + 8) % 8
             shares.append(remote(
-                turned.at[z2 % 2 * 2 + k2, theirs], frames(left_ref.at[slots]),
+                turned.at[z2 % 2 * 2 + k2, theirs], left_ref.at[slots, :, x, y, group],
                 e_send.at[n, i], e_recv.at[n, j], device(x, y, z2, k2)))
-    own.append(pltpu.make_async_copy(natural.at[slab], right_ref.at[me], own_sem.at[3]))
+    own_right = pltpu.make_async_copy(natural.at[slab], right_ref.at[me], own_sem)
     mate = device(x, y, z, k + 1)
     rights = []
     for i, dz in enumerate(hops):
@@ -190,36 +167,47 @@
         handed.append(remote(at, at, r_send.at[4 + i], r_recv.at[4 + i], mate))
 
     features(0)
-    for copy in own[:2] + shares[:14]:
+    for copy in shares[:14]:
         copy.start()
     features(1)
-    for copy in own[2:] + shares[14:] + rights:
-        copy.start()
-    for copy in own[:3]:
-        copy.wait()
+    left_ref[0, :, x, y, 0] = turned[row, slab]
+    left_ref[1:7, :, x, y, 0] = turned[row, 2:8]
 
     px, mx, py, my = along_x[0], along_x[1], along_y[0], along_y[1]
     xp, xm, yp, ym = (x + 1) % 4, (x + 3) % 4, (y + 1) % 4, (y + 3) % 4
 
     def copies(slot, number):
-        half0, half1 = left_ref.at[slot, 0], left_ref.at[slot, 1]
+        if slot is OWN:
+            def part(h, at_x, at_y, half=None):
+                slots = {None: pl.ds(0, 7), 0: pl.ds(0, 4), 1: pl.ds(4, 3)}[half]
+                return left_ref.at[slots, h, at_x, at_y, 0]
+        else:
+            def part(h, at_x, at_y, half=None):
+                groups = {None: pl.ds(1, 7), 0: pl.ds(1, 3), 1: pl.ds(4, 4)}[half]
+                return left_ref.at[slot, h, at_x, at_y, groups]
+        low, high = pl.ds(0, 2), pl.ds(2, 2)
         if number == 0:
-            pairs = [(half0.at[x, y], px), (half0.at[x, y], mx), (half1.at[x, y], py), (half1.at[x, y], my)]
+            pairs = [(part(0, x, y), px), (part(0, x, y), mx), (part(1, x, y), py), (part(1, x, y), my)]
         elif number == 1:
-            pairs = [(half0.at[xm, y, 0], px), (half0.at[xp, y, 1], mx),
-                     (half1.at[x, ym, 0], py), (half1.at[x, yp, 1], my)]
+            pairs = [(part(0, xm, y, 0), px), (part(0, xp, y, 1), mx), (part(1, x, ym, 0), py), (part(1, x, yp, 1), my)]
         elif number == 2:
-            pairs = [(half0.at[:, y], py), (half0.at[:, y], my), (half1.at[x], px), (half1.at[x], mx)]
+            pairs = [(part(0, low, y), py), (part(0, high, y), my), (part(1, x, low), px), (part(1, x, high), mx)]
+        elif number == 3:
+            pairs = [(part(0, low, ym), py), (part(0, high, yp), my), (part(1, xm, low), px), (part(1, xp, high), mx)]
         else:
-            pairs = [(half0.at[pl.ds(0, 2), ym], py), (half0.at[pl.ds(2, 2), yp], my),
-                     (half1.at[xm, pl.ds(0, 2)], px), (half1.at[xp, pl.ds(2, 2)], mx)]
+            pairs = [(part(0, high, y), py), (part(0, low, y), my), (part(1, x, high), px), (part(1, x, low), mx)]
+        at = 7 if slot is OWN else slot
         return [
-            remote(ref, ref, g_send.at[slot, number, i], g_recv.at[slot, number, i], target)
+            remote(ref, ref, g_send.at[at, number, i], g_recv.at[at, number, i], target)
             for i, (ref, target) in enumerate(pairs)
         ]
 
-    def crossing(h):
-        return remote(left_ref.at[0, h], left_ref.at[7, h], x_send.at[h], x_recv.at[h], device(x, y, z + 2, k))
+    def crossing(h, half):
+        return remote(
+            left_ref.at[0, h, :, :, pl.ds(half * 4, 4)], left_ref.at[7, h, :, :, pl.ds(4 - half * 4, 4)],
+            x_send.at[h, half], x_recv.at[h, half], device(x, y, z + 2, k))
+
+    crossings = [crossing(h, half) for h in range(2) for half in range(2)]
 
     def wait_shares(n):
         for copy in shares[n * 7:(n + 1) * 7]:
@@ -235,30 +223,36 @@
                     part = total[c * 32:(c + 1) * 32, a * 128:(a + 1) * 128]
                     out_ref[b, c, quarter, pl.ds(a, 32, stride=4), :] = part
 
+    def advance(slot, number):
+        if number < 5:
+            if number > 0:
+                for copy in copies(slot, number - 1):
+                    copy.wait_recv()
+            elif slot is not OWN:
+                for n, at in enumerate((0, 1, 3)):
+                    pl.when(slot == at)(functools.partial(wait_shares, n))
+            for sent in (2, 4) if number == 2 else (number,):
+                for copy in copies(slot, sent):
+                    copy.start()
+            return
+        for sent in (4, 3):
+            for copy in copies(slot, sent):
+                copy.wait_recv()
+        if slot is not OWN:
+            @pl.when(slot == 0)
+            def _():
+                for copy in crossings:
+                    copy.start()
+
+        for sent in range(5):
+            for copy in copies(slot, sent):
+                copy.wait_send()
+
     def rounds(step, _):
-        for number, lead in ((2, 3), (3, 4), (1, 1), (0, 0), (4, 5)):
-            slot = step - lead
-
-            @pl.when(jnp.logical_and(slot >= 0, slot < 7))
-            def _():
-                if number > 0:
-                    for copy in copies(slot, number - 1):
-                        copy.wait_recv()
-                if number == 0:
-                    for n, at in enumerate((0, 1, 3)):
-                        pl.when(slot == at)(functools.partial(wait_shares, n))
-                if number < 4:
-                    for copy in copies(slot, number):
-                        copy.start()
-                else:
-                    @pl.when(slot == 0)
-                    def _():
-                        for h in range(2):
-                            crossing(h).start()
-
-                    for earlier in range(4):
-                        for copy in copies(slot, earlier):
-                            copy.wait_send()
+        for number, lead in ((0, 0), (1, 1), (2, 2), (3, 3), (5, 4)):
+            slot = step - lead - 1
+            pl.when(slot == -1)(functools.partial(advance, OWN, number))
+            pl.when(jnp.logical_and(slot >= 0, slot < 7))(functools.partial(advance, slot, number))
         return 0
 
     def job(n, _):
@@ -266,8 +260,8 @@
 
         @pl.when(n == 5)
         def _():
-            for h in range(2):
-                crossing(h).wait_recv()
+            for copy in crossings:
+                copy.wait_recv()
 
         multiply(slot, jnp.where(slot == 7, 1 - slab, jnp.where(slot == 0, slab, slot + 1)))
         return 0
@@ -279,29 +273,33 @@
         lax.fori_loop(begin, end, job, 0)
         return 0
 
-    lax.fori_loop(0, 6, rounds, 0)
+    lax.fori_loop(0, 1, rounds, 0)
+    for copy in shares[14:] + rights:
+        copy.start()
+    own_right.start()
+    lax.fori_loop(1, 6, rounds, 0)
     for copy in rights[:3]:
         copy.wait_recv()
     for copy in handed:
         copy.start()
     lax.fori_loop(6, 7, rounds, 0)
-    own[3].wait()
+    own_right.wait()
     rights[3].wait_recv()
     for copy in handed:
         copy.wait_recv()
-    right_columns(right_ref, segment_ref, columns, scale)
+    right_columns(right_ref, segment_ref, columns, scale, me)
     for copy in first + second + shares + rights + handed:
         copy.wait_send()
     lax.fori_loop(7, 11, later, 0)
-    for h in range(2):
-        crossing(h).wait_send()
+    for copy in crossings:
+        copy.wait_send()
     lax.fori_loop(11, 12, rounds, 0)
 
 
 def chunk_rows(left_ref, slot):
     return jnp.concatenate(
         [
-            jnp.concatenate([left_ref[slot, h, x, y, f] for f in range(2)], 1)
+            jnp.concatenate([left_ref[slot, h, x, y, g] for g in range(8)], 1)
             for x in range(4) for y in range(4) for h in range(2)
         ],
         0,
@@ -314,21 +312,25 @@
     return jnp.where((pltpu.roll(ids, LAG, 1) == ids) & (frame >= LAG), 1.0, 0.0)[0:1]
 
 
-def right_columns(right_ref, segment_ref, columns, scale):
+def right_columns(right_ref, segment_ref, columns, scale, me):
     paired = paired_before(segment_ref)
     scale[0] = 1.0 / jnp.sum(paired)
-    for g in range(8):
-        for a in range(4):
-            columns[g * 128:(g + 1) * 128, a * 128:(a + 1) * 128] = right_ref[g, a]
+
+    def wide(g):
+        return jnp.concatenate([right_ref[g, a] for a in range(4)], 1)
+
     for n in range(8):
-        start = min(n * 128, 768)
+        at = pl.ds(pl.multiple_of((n - me + 8) % 8 * 128, 128), 128)
+        columns[at, 0:512] = wide(n)
+        g = min(n, 6)
         here = lax.broadcasted_iota(jnp.int32, (128, 256), 0) + n * 128
-        there = lax.broadcasted_iota(jnp.int32, (128, 256), 1) + start
-        take = jnp.where(there == here + LAG, paired[:, start:start + 256], 0.0).astype(jnp.bfloat16)
-        moved = jnp.dot(take, columns[start:start + 256, 0:512], preferred_element_type=jnp.float32)
-        columns[n * 128:(n + 1) * 128, 512:1024] = moved.astype(jnp.bfloat16)
-
-
+        there = lax.broadcasted_iota(jnp.int32, (128, 256), 1) + g * 128
+        take = jnp.where(there == here + LAG, paired[:, g * 128:g * 128 + 256], 0.0).astype(jnp.bfloat16)
+        both = jnp.concatenate([wide(g), wide(g + 1)], 0)
+        columns[at, 512:1024] = jnp.dot(take, both, preferred_element_type=jnp.float32).astype(jnp.bfloat16)
+
+
+OWN = "own"
 TILES = (2, 16, 4, 128, 128)
 
 
@@ -342,7 +344,7 @@
         out_shape=(
             pltpu.VMEM(TILES, f32),
             pltpu.VMEM(TILES, f32),
-            pltpu.VMEM((8, 2, 4, 4, 2, 16, 512), bf16),
+            pltpu.VMEM((8, 2, 4, 4, 8, 16, 128), bf16),
             pltpu.VMEM((1024, 1024), bf16),
         ),
         in_specs=[anywhere] * 4,
@@ -353,26 +355,25 @@
             pltpu.VMEM((1, 1024), jnp.int32),
             pltpu.VMEM((32768, 128), bf16),
             pltpu.VMEM((4, 4096, 256), bf16),
-            pltpu.VMEM((2, 2, 4, 4, 16, 512), bf16),
+            pltpu.VMEM((2, 4, 4, 16, 1024), bf16),
             pltpu.VMEM((128, 4096), bf16),
-            pltpu.VMEM((4, 128, 256), f32),
             pltpu.VMEM((2, 4, 128, 128), bf16),
             pltpu.VMEM((4, 8, 2, 16, 128), bf16),
             pltpu.VMEM((8, 4, 128, 128), bf16),
             pltpu.SMEM((1,), f32),
             dma((3,)),
             dma((8,)),
-            dma((2, 9)),
-            dma((2, 9)),
+            dma((2, 15)),
+            dma((2, 15)),
             dma((3, 7)),
             dma((3, 7)),
             dma((7,)),
             dma((7,)),
-            dma((7, 4, 4)),
-            dma((7, 4, 4)),
-            dma((2,)),
-            dma((2,)),
-            dma((4,)),
+            dma((8, 5, 4)),
+            dma((8, 5, 4)),
+            dma((2, 2)),
+            dma((2, 2)),
+            dma,
         ],
         compiler_params=pltpu.CompilerParams(
             collective_id=0, has_side_effects=True, vmem_limit_bytes=36 * MIB

time: 79.8 us -> 76.4 us (0.957)
  Pallas kernels: 79.1 us -> 75.6 us
    pallas_call x1, Pallas kernels: 73.2 us -> 69.7 us  [gather(): pl.pallas_call(gather_kernel, out_shape=(pltpu.VMEM(TILES, f32), pltpu.VM...]
where the time goes in v3:
time: 76.4 us; the launch traced here: 76.3 us
  Pallas kernels  75.6 us (99%)
    pallas_call x1, Pallas kernels, gather(): pl.pallas_call(gather_kernel, out_shape=(pltpu.VMEM(TILES, f32), pltpu.VM...  69.7 us
    pallas_call x1, Pallas kernels, finish(): pl.pallas_call(finish_kernel, out_shape=(out, out), in_specs=[vmem] * 5,...  5.87 us

profile of v3, /device:TPU:0, one launch (start us, length us, event | category | flops | bytes accessed | tf_op | source)
XLA Modules:
  0.0 76.3 jit_solution(15501316708340015710)
XLA Ops:
  0.6 0.0 copy-start
  0.6 69.7 %gather_features.1 = (f32[2,16,4,128,128]{4,3,2,1,0:T(8,128)S(1)}, f32[2,16,4,128,128]{4,3,2,1,0:T(8,128)S(1)}, bf16[8,2,4,4,8,16,128]{6,5,4,3,2,1,0:T(8,128)(2,1)S(1)}, bf16[1024,1024]{1,0:T(8,128)(2,1)S(1)}) custom-call(bf16[8,4096]{1,0:T(8,128)(2,1)} %d_hbm.1, bf16[32768,128]{1,0:T(8,128)(2,1)} %bitcast.10, f32[4,2,128]{2,1,0:T(2,128)} %phase_hbm.1, ...), custom_call_target="tpu_custom_call" | custom-call | tf_op jit(solution)/shard_map/gather_features/pallas_call | solution.py:342
  70.4 0.0 copy-done
  70.4 5.9 %covariances.1 = (f32[2,16,4,128,128]{4,3,2,1,0:T(8,128)}, f32[2,16,4,128,128]{4,3,2,1,0:T(8,128)}) custom-call(f32[2,16,4,128,128]{4,3,2,1,0:T(8,128)S(1)} %get-tuple-element.8.instant_tiles, f32[2,16,4,128,128]{4,3,2,1,0:T(8,128)S(1)} %get-tuple-element.9.lagged_tiles, bf16[8,2,4,4,8,16,128]{6,5,4,3,2,1,0:T(8,128)(2,1)S(1)} %get-tuple-element.10.left_ref, ...), custom_call_target="tpu_custom_call" | custom-call | tf_op jit(solution)/shard_map/covariances/pallas_call | solution.py:419
Async XLA Ops:
  0.6 69.8 %copy-start = (s32[1024]{0:T(1024)S(1)}, s32[1024]{0:T(1024)}, u32[]{:S(2)}) copy-start(s32[1024]{0:T(1024)} %param.7) | copy-start | bytes 12292

commit v4 on v3

--- a/solution.py
+++ b/solution.py
@@ -43,26 +43,30 @@
     )
 
 
+def taken(view, sem):
+    pltpu.make_async_copy(view, view, sem).wait()
+
+
 def gather_kernel(
     d_hbm, p_ref, phase_hbm, segment_hbm, instant_ref, lagged_ref, left_ref, columns,
-    d_ref, phase_ref, segment_ref, stage, planes, d_all, d_rows, natural, turned, right_ref, scale,
-    in_sem, p_sem, d_send, d_recv, e_send, e_recv, r_send, r_recv, g_send, g_recv, x_send, x_recv, own_sem,
+    phase_ref, segment_ref, stage, planes, d_all, d_rows, natural, turned, right_ref, scale,
+    in_sem, p_sem, d_sem, first_recv, e_send, e_recv, r_sem, g_send, g_recv, x_sem, own_sem,
 ):
     x, y, z, k = positions()
     me, slab, row = z * 2 + k, z // 2, z % 2 * 2 + k
-    n_chunk = 8
+    n_chunk = 4
     chunk = p_ref.shape[0] // n_chunk
 
     def p_copy(n):
         rows = pl.ds(n * chunk, chunk)
         return pltpu.make_async_copy(p_ref.at[rows], stage.at[rows], p_sem.at[n])
 
-    d_copy = pltpu.make_async_copy(d_hbm, d_ref, in_sem.at[0])
-    phase_copy = pltpu.make_async_copy(phase_hbm, phase_ref, in_sem.at[1])
-    segment_copy = pltpu.make_async_copy(segment_hbm, segment_ref, in_sem.at[2])
-    d_copy.start()
-    phase_copy.start()
-    segment_copy.start()
+    phase_copy = pltpu.make_async_copy(phase_hbm, phase_ref, in_sem.at[0])
+    segment_copy = pltpu.make_async_copy(segment_hbm, segment_ref, in_sem.at[1])
+    own_depth = [d_hbm.at[:, pl.ds(h * 2048, 2048)] for h in range(2)]
+    d_copies = [pltpu.make_async_copy(own_depth[h], d_all.at[h, x, y], in_sem.at[2]) for h in range(2)]
+    for copy in d_copies + [phase_copy, segment_copy]:
+        copy.start()
     for n in range(n_chunk):
         p_copy(n).start()
 
@@ -75,30 +79,24 @@
     for partner in partners:
         pl.semaphore_signal(barrier, inc=1, device_id=partner, device_id_type=MESH)
 
-    d_copy.wait()
+    pl.semaphore_wait(barrier, len(partners))
+
+    axes = (along_x, along_y)
+
+    def send_block(h, source, block, line, recv):
+        for i in range(3):
+            remote(source, block, d_sem.at[0 if recv is None else 1], d_sem.at[2] if recv is None else recv(h, i), line[i]).start()
+
     for h in range(2):
-        low = d_ref[:, h * 1024:(h + 1) * 1024].astype(jnp.float32)
-        high = d_ref[:, 2048 + h * 1024:2048 + (h + 1) * 1024].astype(jnp.float32)
-        d_all[h, x, y] = jnp.concatenate([low, high], 0).astype(jnp.bfloat16)
-    pl.semaphore_wait(barrier, len(partners))
-
-    axes = (along_x, along_y)
-
-    def send_block(h, block_x, block_y, line, n):
-        block = d_all.at[h, block_x, block_y]
-        copies = [remote(block, block, d_send.at[h, n + i], d_recv.at[h, n + i], line[i]) for i in range(3)]
-        for copy in copies:
-            copy.start()
-        return copies
-
-    first = [send_block(h, x, y, axes[h], 0) for h in range(2)]
-    second = [copy for h in range(2) for copy in send_block(h, x, y, axes[1 - h], 3)]
+        send_block(h, own_depth[h], d_all.at[h, x, y], axes[h], lambda h, i: first_recv.at[h, i])
+    for h in range(2):
+        send_block(h, own_depth[h], d_all.at[h, x, y], axes[1 - h], None)
     for i, hop in enumerate(hops):
         for h in range(2):
-            first[h][i].wait_recv()
             from_x, from_y = ((x - hop) % 4, y) if h == 0 else (x, (y - hop) % 4)
-            second += send_block(h, from_x, from_y, axes[1 - h], 6 + 3 * i)
-    first = first[0] + first[1]
+            block = d_all.at[h, from_x, from_y]
+            taken(block, first_recv.at[h, i])
+            send_block(h, block, block, axes[1 - h], None)
 
     to = lax.broadcasted_iota(jnp.int32, (256, 256), 0)
     source = lax.broadcasted_iota(jnp.int32, (256, 256), 1)
@@ -118,20 +116,18 @@
 
     def sort_chunk(n, _):
         p_copy(n).wait()
-        for i in range(4):
-            sort_rows(n * 4 + i)
+        for i in range(8):
+            sort_rows(n * 8 + i)
         return 0
 
     lax.fori_loop(0, n_chunk, sort_chunk, 0)
     phase_copy.wait()
     segment_copy.wait()
-    for copy in second:
-        copy.wait_recv()
+    taken(d_all.at[:, 0:3], d_sem.at[2])
+    taken(d_all.at[:, x, y], in_sem.at[2])
     for h in range(2):
-        for q in range(2):
-            part = d_all[h].astype(jnp.float32).reshape(16, 16, 1024)[:, q * 8:(q + 1) * 8, :]
-            at = q * 2048 + h * 1024
-            d_rows[:, at:at + 1024] = part.reshape(128, 1024).astype(jnp.bfloat16)
+        part = d_all[h].astype(jnp.float32).reshape(128, 2048)
+        d_rows[:, h * 2048:(h + 1) * 2048] = part.astype(jnp.bfloat16)
 
     def features(b):
         for p in range(2):
@@ -146,25 +142,23 @@
     shares = []
     for n, (slots, chunks) in enumerate(batches):
         for i, (dz, dk) in enumerate(mates):
-            j = mates.index((-dz % 4, dk))
             z2, k2 = (z + dz) % 4, (k + dk) % 2
             theirs = pl.ds(z2 // 2, 1) if chunks is None else chunks
             group = (me - (z2 * 2 + k2) + 8) % 8
             shares.append(remote(
                 turned.at[z2 % 2 * 2 + k2, theirs], left_ref.at[slots, :, x, y, group],
-                e_send.at[n, i], e_recv.at[n, j], device(x, y, z2, k2)))
+                e_send.at[n], e_recv.at[n], device(x, y, z2, k2)))
     own_right = pltpu.make_async_copy(natural.at[slab], right_ref.at[me], own_sem)
     mate = device(x, y, z, k + 1)
     rights = []
     for i, dz in enumerate(hops):
         target = device(x, y, z + dz, k)
-        rights.append(remote(
-            natural.at[(z + dz) % 4 // 2], right_ref.at[me], r_send.at[i], r_recv.at[hops.index(-dz % 4)], target))
-    rights.append(remote(natural.at[slab], right_ref.at[me], r_send.at[3], r_recv.at[3], mate))
+        rights.append(remote(natural.at[(z + dz) % 4 // 2], right_ref.at[me], r_sem.at[0], r_sem.at[1], target))
+    rights.append(remote(natural.at[slab], right_ref.at[me], r_sem.at[0], r_sem.at[2], mate))
     handed = []
     for i, dz in enumerate(hops):
         at = right_ref.at[(z + dz) % 4 * 2 + k]
-        handed.append(remote(at, at, r_send.at[4 + i], r_recv.at[4 + i], mate))
+        handed.append(remote(at, at, r_sem.at[3], r_sem.at[2], mate))
 
     features(0)
     for copy in shares[:14]:
@@ -196,22 +190,32 @@
             pairs = [(part(0, low, ym), py), (part(0, high, yp), my), (part(1, xm, low), px), (part(1, xp, high), mx)]
         else:
             pairs = [(part(0, high, y), py), (part(0, low, y), my), (part(1, x, high), px), (part(1, x, low), mx)]
-        at = 7 if slot is OWN else slot
-        return [
-            remote(ref, ref, g_send.at[at, number, i], g_recv.at[at, number, i], target)
-            for i, (ref, target) in enumerate(pairs)
-        ]
+        place = order(slot)
+        send, recv = g_send.at[place % 2, number], g_recv.at[place, number]
+        return [remote(ref, ref, send, recv, target) for ref, target in pairs]
+
+    def order(slot):
+        return 0 if slot is OWN else slot + 1
+
+    def whole(number):
+        blocks = left_ref.at[0, 0, :, :, pl.ds(1, 7)]
+        return (blocks.at[0], blocks.at[0, 0:2], blocks.at[0:2], blocks.at[0:2], blocks.at[0:2])[number]
+
+    def received(slot, number):
+        taken(whole(number), g_recv.at[order(slot), number])
 
     def crossing(h, half):
         return remote(
             left_ref.at[0, h, :, :, pl.ds(half * 4, 4)], left_ref.at[7, h, :, :, pl.ds(4 - half * 4, 4)],
-            x_send.at[h, half], x_recv.at[h, half], device(x, y, z + 2, k))
+            x_sem.at[0], x_sem.at[1], device(x, y, z + 2, k))
 
     crossings = [crossing(h, half) for h in range(2) for half in range(2)]
 
+    def exchanged(n):
+        return left_ref.at[batches[n][0], :, x, y, pl.ds(1, 7)]
+
     def wait_shares(n):
-        for copy in shares[n * 7:(n + 1) * 7]:
-            copy.wait_recv()
+        taken(exchanged(n), e_recv.at[n])
 
     def multiply(slot, number):
         b, quarter = number // 4, number % 4
@@ -226,74 +230,79 @@
     def advance(slot, number):
         if number < 5:
             if number > 0:
-                for copy in copies(slot, number - 1):
-                    copy.wait_recv()
+                received(slot, number - 1)
             elif slot is not OWN:
                 for n, at in enumerate((0, 1, 3)):
                     pl.when(slot == at)(functools.partial(wait_shares, n))
             for sent in (2, 4) if number == 2 else (number,):
+                if slot is not OWN:
+                    @pl.when(slot >= 1)
+                    def _():
+                        taken(whole(sent), g_send.at[order(slot) % 2, sent])
+
                 for copy in copies(slot, sent):
                     copy.start()
             return
         for sent in (4, 3):
-            for copy in copies(slot, sent):
-                copy.wait_recv()
+            received(slot, sent)
         if slot is not OWN:
             @pl.when(slot == 0)
             def _():
                 for copy in crossings:
                     copy.start()
 
-        for sent in range(5):
-            for copy in copies(slot, sent):
-                copy.wait_send()
-
-    def rounds(step, _):
-        for number, lead in ((0, 0), (1, 1), (2, 2), (3, 3), (5, 4)):
-            slot = step - lead - 1
+    def rounds(numbers, step, _):
+        for number in numbers:
+            slot = step - min(number, 4) - 1
             pl.when(slot == -1)(functools.partial(advance, OWN, number))
             pl.when(jnp.logical_and(slot >= 0, slot < 7))(functools.partial(advance, slot, number))
         return 0
 
+    early = functools.partial(rounds, (1, 0, 2, 3))
+    steady = functools.partial(rounds, (0, 1, 2, 3, 5))
+
     def job(n, _):
         slot = n + jnp.where(n == 5, 2, 0) - jnp.where(n == 6, 1, 0)
 
         @pl.when(n == 5)
         def _():
-            for copy in crossings:
-                copy.wait_recv()
+            taken(left_ref.at[7], x_sem.at[1])
 
         multiply(slot, jnp.where(slot == 7, 1 - slab, jnp.where(slot == 0, slab, slot + 1)))
         return 0
 
     def later(step, _):
-        rounds(step, 0)
-        begin = jnp.minimum(2 * (step - 7), 5)
-        end = jnp.where(step == 10, 7, jnp.minimum(2 * (step - 6), 5))
+        steady(step, 0)
+        begin = step - 6 + jnp.where(step >= 8, 1, 0)
+        end = step - 5 + jnp.where(step >= 7, 1, 0) + jnp.where(step == 10, 1, 0)
         lax.fori_loop(begin, end, job, 0)
         return 0
 
-    lax.fori_loop(0, 1, rounds, 0)
+    lax.fori_loop(0, 1, early, 0)
     for copy in shares[14:] + rights:
         copy.start()
     own_right.start()
-    lax.fori_loop(1, 6, rounds, 0)
-    for copy in rights[:3]:
-        copy.wait_recv()
+    lax.fori_loop(1, 4, early, 0)
+    lax.fori_loop(4, 5, steady, 0)
+    taken(right_ref.at[0:3], r_sem.at[1])
     for copy in handed:
         copy.start()
-    lax.fori_loop(6, 7, rounds, 0)
+    lax.fori_loop(5, 6, steady, 0)
     own_right.wait()
-    rights[3].wait_recv()
-    for copy in handed:
-        copy.wait_recv()
+    taken(right_ref.at[0:4], r_sem.at[2])
     right_columns(right_ref, segment_ref, columns, scale, me)
-    for copy in first + second + shares + rights + handed:
-        copy.wait_send()
-    lax.fori_loop(7, 11, later, 0)
-    for copy in crossings:
-        copy.wait_send()
-    lax.fori_loop(11, 12, rounds, 0)
+    taken(d_all.at[:, 0, 0:3], d_sem.at[1])
+    taken(d_all.at[:, 0:3], d_sem.at[0])
+    for n in range(3):
+        taken(exchanged(n), e_send.at[n])
+    taken(right_ref.at[0:4], r_sem.at[0])
+    taken(right_ref.at[0:3], r_sem.at[3])
+    lax.fori_loop(6, 11, later, 0)
+    taken(left_ref.at[7], x_sem.at[0])
+    lax.fori_loop(11, 12, steady, 0)
+    for place in range(2):
+        for number in range(5):
+            taken(whole(number), g_send.at[place, number])
 
 
 def chunk_rows(left_ref, slot):
@@ -350,29 +359,26 @@
         in_specs=[anywhere] * 4,
         out_specs=(vmem,) * 4,
         scratch_shapes=[
-            pltpu.VMEM((8, 4096), bf16),
             pltpu.VMEM((4, 2, 128), f32),
             pltpu.VMEM((1, 1024), jnp.int32),
             pltpu.VMEM((32768, 128), bf16),
             pltpu.VMEM((4, 4096, 256), bf16),
-            pltpu.VMEM((2, 4, 4, 16, 1024), bf16),
+            pltpu.VMEM((2, 4, 4, 8, 2048), bf16),
             pltpu.VMEM((128, 4096), bf16),
             pltpu.VMEM((2, 4, 128, 128), bf16),
             pltpu.VMEM((4, 8, 2, 16, 128), bf16),
             pltpu.VMEM((8, 4, 128, 128), bf16),
             pltpu.SMEM((1,), f32),
             dma((3,)),
-            dma((8,)),
-            dma((2, 15)),
-            dma((2, 15)),
-            dma((3, 7)),
-            dma((3, 7)),
-            dma((7,)),
-            dma((7,)),
-            dma((8, 5, 4)),
-            dma((8, 5, 4)),
-            dma((2, 2)),
-            dma((2, 2)),
+            dma((4,)),
+            dma((3,)),
+            dma((2, 3)),
+            dma((3,)),
+            dma((3,)),
+            dma((4,)),
+            dma((2, 5)),
+            dma((8, 5)),
+            dma((2,)),
             dma,
         ],
         compiler_params=pltpu.CompilerParams(

time: 76.4 us -> 73.1 us (0.957)
  Pallas kernels: 75.6 us -> 72.4 us
    pallas_call x1, Pallas kernels: 69.7 us -> 66.5 us  [gather(): pl.pallas_call(gather_kernel, out_shape=(pltpu.VMEM(TILES, f32), pltpu.VM...]
where the time goes in v4:
time: 73.1 us; the launch traced here: 73 us
  Pallas kernels  72.4 us (99%)
    pallas_call x1, Pallas kernels, gather(): pl.pallas_call(gather_kernel, out_shape=(pltpu.VMEM(TILES, f32), pltpu.VM...  66.5 us
    pallas_call x1, Pallas kernels, finish(): pl.pallas_call(finish_kernel, out_shape=(out, out), in_specs=[vmem] * 5,...  5.87 us

profile of v4, /device:TPU:0, one launch (start us, length us, event | category | flops | bytes accessed | tf_op | source)
XLA Modules:
  0.0 73.0 jit_solution(9219549678865338328)
XLA Ops:
  0.6 0.0 copy-start
  0.6 66.5 %gather_features.1 = (f32[2,16,4,128,128]{4,3,2,1,0:T(8,128)S(1)}, f32[2,16,4,128,128]{4,3,2,1,0:T(8,128)S(1)}, bf16[8,2,4,4,8,16,128]{6,5,4,3,2,1,0:T(8,128)(2,1)S(1)}, bf16[1024,1024]{1,0:T(8,128)(2,1)S(1)}) custom-call(bf16[8,4096]{1,0:T(8,128)(2,1)} %d_hbm.1, bf16[32768,128]{1,0:T(8,128)(2,1)} %bitcast.10, f32[4,2,128]{2,1,0:T(2,128)} %phase_hbm.1, ...), custom_call_target="tpu_custom_call" | custom-call | tf_op jit(solution)/shard_map/gather_features/pallas_call | solution.py:351
  67.1 0.0 copy-done
  67.1 5.9 %covariances.1 = (f32[2,16,4,128,128]{4,3,2,1,0:T(8,128)}, f32[2,16,4,128,128]{4,3,2,1,0:T(8,128)}) custom-call(f32[2,16,4,128,128]{4,3,2,1,0:T(8,128)S(1)} %get-tuple-element.8.instant_tiles, f32[2,16,4,128,128]{4,3,2,1,0:T(8,128)S(1)} %get-tuple-element.9.lagged_tiles, bf16[8,2,4,4,8,16,128]{6,5,4,3,2,1,0:T(8,128)(2,1)S(1)} %get-tuple-element.10.left_ref, ...), custom_call_target="tpu_custom_call" | custom-call | tf_op jit(solution)/shard_map/covariances/pallas_call | solution.py:425
Async XLA Ops:
  0.6 66.5 %copy-start = (s32[1024]{0:T(1024)S(1)}, s32[1024]{0:T(1024)}, u32[]{:S(2)}) copy-start(s32[1024]{0:T(1024)} %param.7) | copy-start | bytes 12292

commit v5 on v4

--- a/solution.py
+++ b/solution.py
@@ -129,14 +129,13 @@
         part = d_all[h].astype(jnp.float32).reshape(128, 2048)
         d_rows[:, h * 2048:(h + 1) * 2048] = part.astype(jnp.bfloat16)
 
-    def features(b):
-        for p in range(2):
-            angles = jnp.dot(d_rows[...], planes[b * 2 + p], preferred_element_type=jnp.float32)
-            for i in range(2):
-                a = p * 2 + i
-                value = cosine(angles[:, i * 128:(i + 1) * 128] + phase_ref[a, b:b + 1])
-                natural[b, a] = value.astype(jnp.bfloat16)
-                turned[a, b * 4:(b + 1) * 4] = value.T.astype(jnp.bfloat16).reshape(4, 2, 16, 128)
+    def features(b, p):
+        angles = jnp.dot(d_rows[...], planes[b * 2 + p], preferred_element_type=jnp.float32)
+        for i in range(2):
+            a = p * 2 + i
+            value = cosine(angles[:, i * 128:(i + 1) * 128] + phase_ref[a, b:b + 1])
+            natural[b, a] = value.astype(jnp.bfloat16)
+            turned[a, b * 4:(b + 1) * 4] = value.T.astype(jnp.bfloat16).reshape(4, 2, 16, 128)
 
     batches = [(pl.ds(0, 1), None), (pl.ds(1, 2), pl.ds(2, 2)), (pl.ds(3, 4), pl.ds(4, 4))]
     shares = []
@@ -160,10 +159,8 @@
         at = right_ref.at[(z + dz) % 4 * 2 + k]
         handed.append(remote(at, at, r_sem.at[3], r_sem.at[2], mate))
 
-    features(0)
-    for copy in shares[:14]:
-        copy.start()
-    features(1)
+    for b in range(2):
+        features(b, row // 2)
     left_ref[0, :, x, y, 0] = turned[row, slab]
     left_ref[1:7, :, x, y, 0] = turned[row, 2:8]
 
@@ -217,10 +214,10 @@
     def wait_shares(n):
         taken(exchanged(n), e_recv.at[n])
 
-    def multiply(slot, number):
+    def multiply(slot, number, count=2):
         b, quarter = number // 4, number % 4
         rows = chunk_rows(left_ref, slot)
-        for out_ref, at, factor in ((instant_ref, 0, 1.0 / 1024), (lagged_ref, 512, scale[0])):
+        for out_ref, at, factor in ((instant_ref, 0, 1.0 / 1024), (lagged_ref, 512, scale[0]))[:count]:
             total = jnp.dot(rows, columns[:, at:at + 512], preferred_element_type=jnp.float32) * factor
             for c in range(16):
                 for a in range(4):
@@ -258,7 +255,7 @@
             pl.when(jnp.logical_and(slot >= 0, slot < 7))(functools.partial(advance, slot, number))
         return 0
 
-    early = functools.partial(rounds, (1, 0, 2, 3))
+    early = functools.partial(rounds, (2, 1, 0, 3))
     steady = functools.partial(rounds, (0, 1, 2, 3, 5))
 
     def job(n, _):
@@ -268,7 +265,14 @@
         def _():
             taken(left_ref.at[7], x_sem.at[1])
 
-        multiply(slot, jnp.where(slot == 7, 1 - slab, jnp.where(slot == 0, slab, slot + 1)))
+        @pl.when(n < 6)
+        def _():
+            multiply(slot, jnp.where(slot == 7, 1 - slab, jnp.where(slot == 0, slab, slot + 1)))
+
+        @pl.when(n == 6)
+        def _():
+            multiply(5, 6, 1)
+
         return 0
 
     def later(step, _):
@@ -278,11 +282,16 @@
         lax.fori_loop(begin, end, job, 0)
         return 0
 
-    lax.fori_loop(0, 1, early, 0)
+    advance(OWN, 0)
+    for b in range(2):
+        features(b, 1 - row // 2)
+    for copy in shares[:14]:
+        copy.start()
+    lax.fori_loop(1, 2, early, 0)
     for copy in shares[14:] + rights:
         copy.start()
     own_right.start()
-    lax.fori_loop(1, 4, early, 0)
+    lax.fori_loop(2, 4, early, 0)
     lax.fori_loop(4, 5, steady, 0)
     taken(right_ref.at[0:3], r_sem.at[1])
     for copy in handed:
@@ -388,11 +397,8 @@
     )(distances, projection, phases, segment_ids)
 
 
-LAST_SLOT, LAST_CHUNK = 6, 7
-
-
 def finish_kernel(
-    instant_tiles, lagged_tiles, left_ref, columns, segment_ref, instant_ref, lagged_ref, instant_last, lagged_last, sem
+    instant_tiles, lagged_tiles, left_ref, columns, segment_ref, instant_ref, lagged_ref, last, sem
 ):
     copies = []
 
@@ -401,19 +407,20 @@
         copy.start()
         copies.append(copy)
 
-    outs = ((instant_tiles, instant_ref, instant_last), (lagged_tiles, lagged_ref, lagged_last))
-    for i, (tiles, out_ref, _) in enumerate(outs):
+    outs = ((instant_tiles, instant_ref), (lagged_tiles, lagged_ref))
+    for i, (tiles, out_ref) in enumerate(outs):
         move(tiles.at[0], out_ref.at[0], i * 3)
-        move(tiles.at[1, :, pl.ds(0, 3)], out_ref.at[1, :, pl.ds(0, 3)], i * 3 + 1)
-    rows = chunk_rows(left_ref, LAST_SLOT)
+        done = pl.ds(0, 3 - i)
+        move(tiles.at[1, :, done], out_ref.at[1, :, done], i * 3 + 1)
     inverse = 1.0 / jnp.sum(paired_before(segment_ref))
-    for i, (_, out_ref, last) in enumerate(outs):
+    for n, (slot, i) in enumerate(((5, 1), (6, 0), (6, 1))):
+        rows = chunk_rows(left_ref, slot)
         total = jnp.dot(rows, columns[:, i * 512:(i + 1) * 512], preferred_element_type=jnp.float32)
         total = total * (inverse if i else 1.0 / 1024)
         for c in range(16):
             for a in range(4):
-                last[c, pl.ds(a, 32, stride=4), :] = total[c * 32:(c + 1) * 32, a * 128:(a + 1) * 128]
-        move(last, out_ref.at[1, :, 3], i * 3 + 2)
+                last[n, c, pl.ds(a, 32, stride=4), :] = total[c * 32:(c + 1) * 32, a * 128:(a + 1) * 128]
+        move(last.at[n], outs[i][1].at[1, :, slot - 3], (2, 5, 6)[n])
     for copy in copies:
         copy.wait()
 
@@ -428,11 +435,10 @@
         in_specs=[vmem] * 5,
         out_specs=(anywhere, anywhere),
         scratch_shapes=[
-            pltpu.VMEM((16, 128, 128), jnp.float32),
-            pltpu.VMEM((16, 128, 128), jnp.float32),
-            pltpu.SemaphoreType.DMA((6,)),
+            pltpu.VMEM((3, 16, 128, 128), jnp.float32),
+            pltpu.SemaphoreType.DMA((7,)),
         ],
-        compiler_params=pltpu.CompilerParams(vmem_limit_bytes=4 * MIB),
+        compiler_params=pltpu.CompilerParams(vmem_limit_bytes=5 * MIB),
         name="covariances",
     )(*tiles, segment_ids)
 

time: 73.1 us -> 72.4 us (level)
  Pallas kernels: 72.4 us -> 71.6 us
    pallas_call x1, Pallas kernels: 66.5 us -> 65.8 us  [gather(): pl.pallas_call(gather_kernel, out_shape=(pltpu.VMEM(TILES, f32), pltpu.VM...]
where the time goes in v5:
time: 72.4 us; the launch traced here: 72.3 us
  Pallas kernels  71.6 us (99%)
    pallas_call x1, Pallas kernels, gather(): pl.pallas_call(gather_kernel, out_shape=(pltpu.VMEM(TILES, f32), pltpu.VM...  65.8 us
    pallas_call x1, Pallas kernels, finish(): pl.pallas_call(finish_kernel, out_shape=(out, out), in_specs=[vmem] * 5,...  5.88 us

profile of v5, /device:TPU:0, one launch (start us, length us, event | category | flops | bytes accessed | tf_op | source)
XLA Modules:
  0.0 72.3 jit_solution(6353173263749756870)
XLA Ops:
  0.6 0.0 copy-start
  0.6 65.8 %gather_features.1 = (f32[2,16,4,128,128]{4,3,2,1,0:T(8,128)S(1)}, f32[2,16,4,128,128]{4,3,2,1,0:T(8,128)S(1)}, bf16[8,2,4,4,8,16,128]{6,5,4,3,2,1,0:T(8,128)(2,1)S(1)}, bf16[1024,1024]{1,0:T(8,128)(2,1)S(1)}) custom-call(bf16[8,4096]{1,0:T(8,128)(2,1)} %d_hbm.1, bf16[32768,128]{1,0:T(8,128)(2,1)} %bitcast.10, f32[4,2,128]{2,1,0:T(2,128)} %phase_hbm.1, ...), custom_call_target="tpu_custom_call" | custom-call | tf_op jit(solution)/shard_map/gather_features/pallas_call | solution.py:360
  66.4 0.0 copy-done
  66.4 5.9 %covariances.1 = (f32[2,16,4,128,128]{4,3,2,1,0:T(8,128)}, f32[2,16,4,128,128]{4,3,2,1,0:T(8,128)}) custom-call(f32[2,16,4,128,128]{4,3,2,1,0:T(8,128)S(1)} %get-tuple-element.8.instant_tiles, f32[2,16,4,128,128]{4,3,2,1,0:T(8,128)S(1)} %get-tuple-element.9.lagged_tiles, bf16[8,2,4,4,8,16,128]{6,5,4,3,2,1,0:T(8,128)(2,1)S(1)} %get-tuple-element.10.left_ref, ...), custom_call_target="tpu_custom_call" | custom-call | tf_op jit(solution)/shard_map/covariances/pallas_call | solution.py:432
Async XLA Ops:
  0.6 65.8 %copy-start = (s32[1024]{0:T(1024)S(1)}, s32[1024]{0:T(1024)}, u32[]{:S(2)}) copy-start(s32[1024]{0:T(1024)} %param.7) | copy-start | bytes 12292

commit v6 on v5

--- a/solution.py
+++ b/solution.py
@@ -217,8 +217,9 @@
     def multiply(slot, number, count=2):
         b, quarter = number // 4, number % 4
         rows = chunk_rows(left_ref, slot)
-        for out_ref, at, factor in ((instant_ref, 0, 1.0 / 1024), (lagged_ref, 512, scale[0]))[:count]:
-            total = jnp.dot(rows, columns[:, at:at + 512], preferred_element_type=jnp.float32) * factor
+        for out_ref, at, factor in ((instant_ref, 0, None), (lagged_ref, 512, scale[0]))[:count]:
+            total = jnp.dot(rows, columns[:, at:at + 512], preferred_element_type=jnp.float32)
+            total = total if factor is None else total * factor
             for c in range(16):
                 for a in range(4):
                     part = total[c * 32:(c + 1) * 32, a * 128:(a + 1) * 128]
@@ -339,7 +340,7 @@
 
     for n in range(8):
         at = pl.ds(pl.multiple_of((n - me + 8) % 8 * 128, 128), 128)
-        columns[at, 0:512] = wide(n)
+        columns[at, 0:512] = (wide(n).astype(jnp.float32) * (1.0 / 1024)).astype(jnp.bfloat16)
         g = min(n, 6)
         here = lax.broadcasted_iota(jnp.int32, (128, 256), 0) + n * 128
         there = lax.broadcasted_iota(jnp.int32, (128, 256), 1) + g * 128
@@ -416,7 +417,7 @@
     for n, (slot, i) in enumerate(((5, 1), (6, 0), (6, 1))):
         rows = chunk_rows(left_ref, slot)
         total = jnp.dot(rows, columns[:, i * 512:(i + 1) * 512], preferred_element_type=jnp.float32)
-        total = total * (inverse if i else 1.0 / 1024)
+        total = total * inverse if i else total
         for c in range(16):
             for a in range(4):
                 last[n, c, pl.ds(a, 32, stride=4), :] = total[c * 32:(c + 1) * 32, a * 128:(a + 1) * 128]

time: 72.4 us -> 72.4 us (level)
  no operation moved by 1% of the time
where the time goes in v6:
time: 72.4 us; the launch traced here: 72.3 us
  Pallas kernels  71.6 us (99%)
    pallas_call x1, Pallas kernels, gather(): pl.pallas_call(gather_kernel, out_shape=(pltpu.VMEM(TILES, f32), pltpu.VM...  65.8 us
    pallas_call x1, Pallas kernels, finish(): pl.pallas_call(finish_kernel, out_shape=(out, out), in_specs=[vmem] * 5,...  5.88 us

profile of v6, /device:TPU:0, one launch (start us, length us, event | category | flops | bytes accessed | tf_op | source)
XLA Modules:
  0.0 72.3 jit_solution(2832459760849320585)
XLA Ops:
  0.6 0.0 copy-start
  0.6 65.8 %gather_features.1 = (f32[2,16,4,128,128]{4,3,2,1,0:T(8,128)S(1)}, f32[2,16,4,128,128]{4,3,2,1,0:T(8,128)S(1)}, bf16[8,2,4,4,8,16,128]{6,5,4,3,2,1,0:T(8,128)(2,1)S(1)}, bf16[1024,1024]{1,0:T(8,128)(2,1)S(1)}) custom-call(bf16[8,4096]{1,0:T(8,128)(2,1)} %d_hbm.1, bf16[32768,128]{1,0:T(8,128)(2,1)} %bitcast.10, f32[4,2,128]{2,1,0:T(2,128)} %phase_hbm.1, ...), custom_call_target="tpu_custom_call" | custom-call | tf_op jit(solution)/shard_map/gather_features/pallas_call | solution.py:361
  66.4 0.0 copy-done
  66.4 5.9 %covariances.1 = (f32[2,16,4,128,128]{4,3,2,1,0:T(8,128)}, f32[2,16,4,128,128]{4,3,2,1,0:T(8,128)}) custom-call(f32[2,16,4,128,128]{4,3,2,1,0:T(8,128)S(1)} %get-tuple-element.8.instant_tiles, f32[2,16,4,128,128]{4,3,2,1,0:T(8,128)S(1)} %get-tuple-element.9.lagged_tiles, bf16[8,2,4,4,8,16,128]{6,5,4,3,2,1,0:T(8,128)(2,1)S(1)} %get-tuple-element.10.left_ref, ...), custom_call_target="tpu_custom_call" | custom-call | tf_op jit(solution)/shard_map/covariances/pallas_call | solution.py:433
Async XLA Ops:
  0.6 65.8 %copy-start = (s32[1024]{0:T(1024)S(1)}, s32[1024]{0:T(1024)}, u32[]{:S(2)}) copy-start(s32[1024]{0:T(1024)} %param.7) | copy-start | bytes 12292
